TPU v7x, 32 devices: a whole 2x2x4 slice. The times are simulated.
32 devices in a mesh: dp: 8 (over y, x, core), head: 4 (over z).
Axes of the slice: x: 2, y: 2, z: 4, core: 2. Of those that a mesh axis runs over, the one named last changes fastest.
Arguments:
- hidden_in: bfloat16 [32, 512, 768], P('dp', 'head'), may hold values from -6 to 6
- cotangent: bfloat16 [32, 512, 768], P('dp', 'head'), may hold values from -6 to 6
- box_coords: int32 [32, 512, 4], P('dp'), may hold values from 0 to 1023
- doc_lengths: int32 [32, 4], P('dp'), may hold values from 1 to 509, as said below
- params: float32 [7700480], P(('dp', 'head')), may hold values from -3 to 3
- moment_one: float32 [7700480], P(('dp', 'head')), may hold values from -60 to 60
- moment_two: float32 [7700480], P(('dp', 'head')), may hold values from 1 to 10000
Outputs:
- output: bfloat16 [32, 512, 768], P('dp', 'head')
- grad_hidden: bfloat16 [32, 512, 768], P('dp', 'head')
- grad_params: float32 [7700480], P(('dp', 'head'))
- param_step: float32 [7700480], P(('dp', 'head'))
- new_moment_one: float32 [7700480], P(('dp', 'head'))
Inputs may be any that keep to these rules, and one draw needn't show every extreme that they name: `doc_lengths`: each row holds the lengths of the 4 documents of one window, summing to 512; the second document starts within the first quarter of the window and ends within its last quarter.
All inputs are finite; a program needn't handle non-finite values.
Results may differ from a plain program's by a relative error of at most 0.019.
Values may be sent and summed in bfloat16 or wider, within the bound.
A program may use at most 192 MiB of HBM per device.

v0:
```python
import functools
import math

import jax
import jax.numpy as jnp
import numpy as np
from jax import lax
from jax.experimental import pallas as pl
from jax.experimental.pallas import tpu as pltpu
from jax.sharding import PartitionSpec as P

D = 768
HEADS = 12
FF = 3072
BUCKETS = 32
WINLEN = 512
HEAD_DIM = 64
PAIRS = HEADS // 2
LANES = 128
BLOCKS = WINLEN // LANES

beta_one = 0.9
beta_two = 0.999
adam_eps = 1e-08
norm_eps = 1e-05
base_rate = 0.001
layer_decay = 0.75
decay_weight = 0.01
adam_count = 100
coord_cell = 32
masked_score = -1e30

F32 = jnp.float32
BF16 = jnp.bfloat16


def layouts_list():
    return (
        (D, 3 * D),
        (D, D),
        (D, D),
        (D, FF),
        (FF, D),
        (2, D),
        (D,),
        (2, D),
        (FF,),
        (D,),
        (2, D),
        (3, HEADS, BUCKETS),
    )


def unpack(flat_params):
    pieces = []
    offset = 0
    for layout in layouts_list():
        elements = math.prod(layout)
        pieces.append(flat_params[offset : offset + elements].reshape(layout))
        offset += elements
    return pieces


def matmul(left_mat, right_mat):
    return jnp.dot(left_mat, right_mat, preferred_element_type=F32)


def rows_inner(left_mat, right_mat):
    return lax.dot_general(left_mat, right_mat, (((0,), (0,)), ((), ())), preferred_element_type=F32)


def times_transposed(left_mat, right_mat):
    return lax.dot_general(left_mat, right_mat, (((1,), (1,)), ((), ())), preferred_element_type=F32)


def layer_norm(values, gain_bias):
    row_mean = jnp.mean(values, axis=-1, keepdims=True)
    centred = values - row_mean
    spread = jnp.mean(centred * centred, axis=-1, keepdims=True)
    return centred * lax.rsqrt(spread + norm_eps) * gain_bias[0] + gain_bias[1]


def gelu_exact(values):
    return jax.nn.gelu(values, approximate=False)


def hot(index, count):
    return (np.asarray(index)[..., None] == np.arange(count)).astype(np.float32)


def clipped(steps):
    return np.clip(steps, -(BUCKETS // 2), BUCKETS // 2 - 1) + BUCKETS // 2


CELLS = np.arange(BUCKETS)
HOT_SAME = hot(clipped(CELLS[:, None] - CELLS[None, :]), BUCKETS)
HOT_LESS = hot(clipped(CELLS[:, None] - CELLS[None, :] - 1), BUCKETS)
WIDE = 6 * LANES
_U = np.arange(WIDE)
BAND_HOT = hot(np.where(_U < 5 * LANES, clipped(_U - 2 * LANES), 0), BUCKETS)
_V = np.arange(4 * LANES)
DIAG_HOT = np.concatenate(
    [
        hot(np.zeros(LANES, np.int64), BUCKETS),
        hot(np.where(_V < 3 * LANES, clipped(_V - LANES), 0), BUCKETS),
        hot(np.full(LANES, BUCKETS - 1), BUCKETS),
    ]
)


def window_layout(doc_lengths, box_coords):
    doc_ends = jnp.cumsum(doc_lengths, dtype=jnp.int32)
    doc_starts = doc_ends - doc_lengths
    places = jnp.arange(WINLEN, dtype=jnp.int32)
    doc_ids = jnp.sum(
        (places[:, None] >= doc_ends[None, :]).astype(jnp.int32), axis=1, dtype=jnp.int32
    )
    docs = jnp.arange(doc_lengths.shape[0], dtype=jnp.int32)
    chosen = doc_ids[:, None] == docs[None, :]
    first_hot = places[:, None] == doc_starts[None, :]
    first_box = jnp.sum(
        jnp.where(first_hot[:, :, None], box_coords[:, None, :], 0), axis=0, dtype=jnp.int32
    )
    anchor = jnp.sum(
        jnp.where(chosen[:, :, None], first_box[None, :, :], 0), axis=1, dtype=jnp.int32
    )
    relative = box_coords - jnp.concatenate([anchor[:, :2], anchor[:, :2]], axis=1)
    centre_x = (box_coords[:, 0] + box_coords[:, 2]) // 2
    centre_y = (box_coords[:, 1] + box_coords[:, 3]) // 2
    return chosen, relative, centre_x, centre_y


def box_features(relative):
    count_freq = D // 8
    steps = jnp.arange(count_freq, dtype=F32)
    frequency = jnp.exp(steps * (-math.log(1000.0) / count_freq))
    angles = relative.astype(F32)[:, :, None] * frequency[None, None, :]
    return jnp.concatenate([jnp.sin(angles), jnp.cos(angles)], axis=2).reshape(relative.shape[0], D)


def bias_operands(tables, chosen, centre_x, centre_y):
    cell_x, cell_y = centre_x // coord_cell, centre_y // coord_cell
    rest_x, rest_y = centre_x % coord_cell, centre_y % coord_cell
    cells = jnp.arange(BUCKETS, dtype=jnp.int32)
    hot_x = (cell_x[:, None] == cells[None, :]).astype(BF16)
    hot_y = (cell_y[:, None] == cells[None, :]).astype(BF16)
    none = jnp.zeros_like(hot_x)
    hot_two = jnp.concatenate([hot_x, hot_y, hot_x, hot_y], axis=1)
    key_x = jnp.stack(
        [
            jnp.concatenate([hot_x, -hot_x, none, none], axis=1),
            jnp.concatenate([none, none, hot_x, -hot_x], axis=1),
        ]
    )
    key_y = jnp.stack(
        [
            jnp.concatenate([hot_y, -hot_y, none, none], axis=1),
            jnp.concatenate([none, none, hot_y, -hot_y], axis=1),
        ]
    )
    same = jnp.einsum("qcb,thb->thqc", HOT_SAME.astype(BF16), tables[1:], preferred_element_type=F32)
    less = jnp.einsum("qcb,thb->thqc", HOT_LESS.astype(BF16), tables[1:], preferred_element_type=F32)
    zero = jnp.zeros_like(same[0])
    base = jnp.concatenate(
        [jnp.concatenate([same[0], zero], axis=2), jnp.concatenate([zero, same[1]], axis=2)], axis=1
    )
    base = base.reshape(PAIRS, 2, 64, 64)[:, ::-1].reshape(HEADS, 64, 64)
    diff_x = jnp.concatenate([jnp.concatenate([less[0], same[0]], axis=2), jnp.zeros((HEADS, 32, 64), F32)], axis=1)
    diff_y = jnp.concatenate([jnp.zeros((HEADS, 32, 64), F32), jnp.concatenate([less[1], same[1]], axis=2)], axis=1)
    rows = jnp.concatenate([base, diff_x, diff_y], axis=0).astype(BF16)
    rows = rows.transpose(1, 0, 2).reshape(64, 3 * D)
    met = matmul(hot_two[:, :64], rows).astype(BF16)
    band = matmul(tables[0], jnp.asarray(BAND_HOT.T, BF16)).reshape(HEADS, 1, WIDE)
    rest_cols = jnp.stack([rest_x, rest_y], axis=1).astype(F32)
    rest_rows = rest_cols.T
    pad = jnp.zeros((WINLEN, LANES - chosen.shape[1]), BF16)
    marks = chosen.astype(BF16)
    mark_keys = jnp.concatenate([marks, pad], axis=1)
    mark_queries = jnp.concatenate([(1 - marks) * jnp.asarray(masked_score, BF16), pad], axis=1)
    return dict(
        hot_two=hot_two,
        key_x=key_x,
        key_y=key_y,
        met=met,
        band=band,
        rest_cols=rest_cols,
        rest_rows=rest_rows,
        mark_keys=mark_keys,
        mark_queries=mark_queries,
    )


def half_masks():
    lane = lax.broadcasted_iota(jnp.int32, (1, LANES), 1)
    low = (lane < HEAD_DIM).astype(F32)
    return low.astype(BF16), (1.0 - low).astype(BF16)


def less_masks(rest_cols, rest_rows, less_x, less_y):
    for part in range(BLOCKS):
        rows = slice(part * LANES, (part + 1) * LANES)
        for axis, less in ((0, less_x), (1, less_y)):
            column = rest_cols[rows, axis : axis + 1]
            row = rest_rows[axis : axis + 1, :]
            less[rows, :] = jnp.where(row < column, 1.0, 0.0).astype(less.dtype)


def attention_forward_kernel(
    q_ref, k_ref, v_ref, hot_ref, keyx_ref, keyy_ref, met_ref, band_ref, cols_ref, rows_ref,
    mkey_ref, mquery_ref, probs_ref, context_ref,
    kaug, qaug, less_x, less_y, wide, scores,
):
    low, high = half_masks()
    less_masks(cols_ref, rows_ref, less_x, less_y)
    kaug[:, LANES:] = mkey_ref[...]
    qaug[:, LANES:] = mquery_ref[...]
    half = 2 * LANES

    def one_pair(pair, carry):
        at = pl.multiple_of(pair * LANES, LANES)
        lanes = pl.ds(at, LANES)
        lanes_x = pl.ds(pl.multiple_of(at + D, LANES), LANES)
        lanes_y = pl.ds(pl.multiple_of(at + 2 * D, LANES), LANES)
        values_t = v_ref[:, lanes].T
        for odd in range(2):
            own, other = (low, high) if odd == 0 else (high, low)
            head = 2 * pair + odd
            kaug[:, :LANES] = k_ref[:, lanes] * own + hot_ref[...] * other
            qaug[:, :LANES] = q_ref[:, lanes] * own + met_ref[:, lanes] * other
            skew_band(band_ref[head], wide)
            for side in range(2):
                cols = slice(side * half, (side + 1) * half)
                top = None
                for part in range(BLOCKS):
                    rows = slice(part * LANES, (part + 1) * LANES)
                    s = times_transposed(kaug[rows, :], qaug[cols, :])
                    dx = times_transposed(keyx_ref[odd, rows, :], met_ref[cols, lanes_x])
                    dy = times_transposed(keyy_ref[odd, rows, :], met_ref[cols, lanes_y])
                    bias = []
                    for block in range(2 * side, 2 * side + 2):
                        step = max(-2, min(2, block - part)) + 2
                        bias.append(wide[:, step * LANES : (step + 1) * LANES])
                    s = s + jnp.concatenate(bias, axis=1)
                    s = s + dx * less_x[rows, cols] + dy * less_y[rows, cols]
                    scores[rows, :] = s
                    best = jnp.max(s, axis=0, keepdims=True)
                    top = best if top is None else jnp.maximum(top, best)
                total = None
                for part in range(BLOCKS):
                    rows = slice(part * LANES, (part + 1) * LANES)
                    e = jnp.exp(scores[rows, :] - top)
                    scores[rows, :] = e
                    add = jnp.sum(e, axis=0, keepdims=True)
                    total = add if total is None else total + add
                share = 1.0 / total
                for part in range(BLOCKS):
                    rows = slice(part * LANES, (part + 1) * LANES)
                    probs_ref[head, rows, cols] = (scores[rows, :] * share).astype(BF16)
                got = matmul(
                    values_t[odd * HEAD_DIM : (odd + 1) * HEAD_DIM, :], probs_ref[head, :, cols]
                )
                context_ref[pl.ds(pl.multiple_of(head * HEAD_DIM, HEAD_DIM), HEAD_DIM), cols] = (
                    got.astype(BF16)
                )
        return carry

    lax.fori_loop(0, PAIRS, one_pair, 0)


def skew_band(row, wide):
    x = jnp.broadcast_to(row, (8, WIDE))
    sub = lax.broadcasted_iota(jnp.int32, (8, WIDE), 0)
    for bit in (1, 2, 4):
        x = jnp.where((sub & bit) != 0, pltpu.roll(x, bit, 1), x)
    for group in range(LANES // 8):
        y = x if group == 0 else pltpu.roll(x, 8 * group, 1)
        wide[8 * group : 8 * group + 8, :] = y[:, : 5 * LANES]


def skew_groups(skewed, wide):
    for group in range(LANES // 8):
        y = skewed if group == 0 else pltpu.roll(skewed, 8 * group, 1)
        wide[8 * group : 8 * group + 8, :] = y[:, : 5 * LANES]


def diagonal_sums(parts):
    total = None
    for group in range(LANES // 8):
        x = jnp.concatenate(
            [parts[8 * group : 8 * group + 8, LANES : 4 * LANES], jnp.zeros((8, LANES), F32)], axis=1
        )
        y = x if group == 0 else pltpu.roll(x, 4 * LANES - 8 * group, 1)
        total = y if total is None else total + y
    sub = lax.broadcasted_iota(jnp.int32, (8, 4 * LANES), 0)
    for bit in (1, 2, 4):
        total = jnp.where((sub & bit) != 0, pltpu.roll(total, 4 * LANES - bit, 1), total)
    return jnp.sum(total, axis=0, keepdims=True)


def attention_backward_kernel(
    q_ref, k_ref, v_ref, dctx_ref, probs_ref, hot_ref, cols_ref, rows_ref,
    dq_ref, dk_ref, dv_ref, cells_ref, diag_ref,
    qaug, less_x, less_y, scores, dscores, band, kept, hot_t,
):
    low, high = half_masks()
    less_masks(cols_ref, rows_ref, less_x, less_y)
    hot_t[...] = hot_ref[...].T
    lane = lax.broadcasted_iota(jnp.int32, (1, LANES), 1)
    scale = HEAD_DIM ** (-0.5)
    of_x = jnp.where((lane // BUCKETS) % 2 == 0, 1.0, 0.0)
    cells_x = hot_ref[...] * of_x.astype(BF16)
    cells_y = hot_ref[...] * (1.0 - of_x).astype(BF16)

    def one_pair(pair, carry):
        at = pl.multiple_of(pair * LANES, LANES)
        lanes = pl.ds(at, LANES)
        keys_t = k_ref[:, lanes].T
        for odd in range(2):
            own, other = (low, high) if odd == 0 else (high, low)
            head = 2 * pair + odd
            qaug[...] = q_ref[:, lanes] * own + hot_ref[...] * other
            dctx = dctx_ref[:, lanes]
            dot = None
            for part in range(BLOCKS):
                rows = slice(part * LANES, (part + 1) * LANES)
                dp = times_transposed(v_ref[rows, lanes] * own, dctx)
                scores[rows, :] = dp
                add = jnp.sum(dp * probs_ref[head, rows, :].astype(F32), axis=0, keepdims=True)
                dot = add if dot is None else dot + add
            band[...] = jnp.zeros_like(band)
            for part in range(BLOCKS):
                rows = slice(part * LANES, (part + 1) * LANES)
                probs = probs_ref[head, rows, :]
                ds = probs.astype(F32) * (scores[rows, :] - dot)
                for block in range(BLOCKS):
                    step = max(-2, min(2, block - part)) + 2
                    where = slice(step * LANES, (step + 1) * LANES)
                    band[:, where] = band[:, where] + ds[:, block * LANES : (block + 1) * LANES]
                ds = ds.astype(BF16)
                dscores[rows, :] = ds
                both = matmul(ds, qaug[...])
                less = matmul(ds * less_x[rows, :], cells_x) + matmul(ds * less_y[rows, :], cells_y)
                dv = matmul(probs, dctx)
                kept[odd, 0, rows, :] = both
                kept[odd, 1, rows, :] = less
                kept[odd, 2, rows, :] = dv
            got = matmul(keys_t[odd * HEAD_DIM : (odd + 1) * HEAD_DIM, :], dscores[...])
            dq_ref[pl.ds(pl.multiple_of(head * HEAD_DIM, HEAD_DIM), HEAD_DIM), :] = (
                got * scale
            ).astype(BF16)
            diag_ref[head, :, LANES : 5 * LANES] = diagonal_sums(band)
            diag_ref[head, :, :LANES] = jnp.sum(band[:, :LANES], axis=0, keepdims=True)
            diag_ref[head, :, 5 * LANES :] = jnp.sum(band[:, 4 * LANES :], axis=0, keepdims=True)
            for which in range(2):
                summed = kept[odd, which]
                first = summed.astype(BF16)
                rest = (summed - first.astype(F32)).astype(BF16)
                cells_ref[head, which] = matmul(hot_t[:64, :], first) + matmul(hot_t[:64, :], rest)
        dk_ref[:, lanes] = jnp.where(lane < HEAD_DIM, kept[0, 0], kept[1, 0]).astype(BF16)
        dv_ref[:, lanes] = jnp.where(lane < HEAD_DIM, kept[0, 2], kept[1, 2]).astype(BF16)
        return carry

    lax.fori_loop(0, PAIRS, one_pair, 0)


def attention_forward(queries, keys, values, ops):
    return pl.pallas_call(
        attention_forward_kernel,
        out_shape=(
            jax.ShapeDtypeStruct((HEADS, WINLEN, WINLEN), BF16),
            jax.ShapeDtypeStruct((D, WINLEN), BF16),
        ),
        scratch_shapes=[
            pltpu.VMEM((WINLEN, 2 * LANES), BF16),
            pltpu.VMEM((WINLEN, 2 * LANES), BF16),
            pltpu.VMEM((WINLEN, WINLEN), F32),
            pltpu.VMEM((WINLEN, WINLEN), F32),
            pltpu.VMEM((LANES, 5 * LANES), F32),
            pltpu.VMEM((WINLEN, 2 * LANES), F32),
        ],
        compiler_params=pltpu.CompilerParams(vmem_limit_bytes=48 * 2**20),
        name="attention_forward",
    )(
        queries, keys, values, ops["hot_two"], ops["key_x"], ops["key_y"], ops["met"], ops["band"],
        ops["rest_cols"], ops["rest_rows"], ops["mark_keys"], ops["mark_queries"],
    )


def attention_backward(queries, keys, values, grad_context, probs, ops):
    return pl.pallas_call(
        attention_backward_kernel,
        out_shape=(
            jax.ShapeDtypeStruct((D, WINLEN), BF16),
            jax.ShapeDtypeStruct((WINLEN, D), BF16),
            jax.ShapeDtypeStruct((WINLEN, D), BF16),
            jax.ShapeDtypeStruct((HEADS, 2, 64, LANES), F32),
            jax.ShapeDtypeStruct((HEADS, 1, WIDE), F32),
        ),
        scratch_shapes=[
            pltpu.VMEM((WINLEN, LANES), BF16),
            pltpu.VMEM((WINLEN, WINLEN), BF16),
            pltpu.VMEM((WINLEN, WINLEN), BF16),
            pltpu.VMEM((WINLEN, WINLEN), F32),
            pltpu.VMEM((WINLEN, WINLEN), BF16),
            pltpu.VMEM((LANES, 5 * LANES), F32),
            pltpu.VMEM((2, 3, WINLEN, LANES), F32),
            pltpu.VMEM((LANES, WINLEN), BF16),
        ],
        compiler_params=pltpu.CompilerParams(vmem_limit_bytes=48 * 2**20),
        name="attention_backward",
    )(
        queries, keys, values, grad_context, probs, ops["hot_two"], ops["rest_cols"],
        ops["rest_rows"],
    )


def table_grads(cells, diag):
    exact = lax.Precision.HIGHEST
    pairs = cells.reshape(PAIRS, 2, 2, 64, LANES)
    every = jnp.stack([pairs[:, 0, 0, :, 64:], pairs[:, 1, 0, :, :64]], axis=1).reshape(HEADS, 64, 64)
    less = cells[:, 1]
    less_x, less_y = less[:, :32, :32], less[:, 32:, 32:64]
    all_x, all_y = every[:, :32, :32], every[:, 32:, 32:]
    same = jnp.stack([all_x - less_x, all_y - less_y]).reshape(2 * HEADS, -1)
    below = jnp.stack([less_x, less_y]).reshape(2 * HEADS, -1)
    same_hot = jnp.asarray(HOT_SAME.transpose(1, 0, 2).reshape(-1, BUCKETS))
    less_hot = jnp.asarray(HOT_LESS.transpose(1, 0, 2).reshape(-1, BUCKETS))
    moved = jnp.dot(same, same_hot, precision=exact) + jnp.dot(below, less_hot, precision=exact)
    along = jnp.dot(diag.reshape(HEADS, WIDE), jnp.asarray(DIAG_HOT), precision=exact)
    return jnp.concatenate([along[None], moved.reshape(2, HEADS, BUCKETS)], axis=0)


COLUMNS = 4
CORES = 2
DEPTH = 4
USED = sum(math.prod(layout) for layout in layouts_list())
MATRICES = layouts_list()[:5]
MISC = sum(math.prod(layout) for layout in layouts_list()[5:])
MISC_ROWS = -(-MISC // (8 * LANES)) * 8


class Plan:
    def __init__(self, shard_len, carry=3 * LANES):
        self.rows = shard_len // LANES
        self.quarter = -(-self.rows // (16 * COLUMNS)) * 16
        self.padded = COLUMNS * self.quarter
        self.per_column = CORES * DEPTH * self.rows
        self.carry = carry
        self.staged = self.carry + self.per_column + 3 * LANES
        starts = []
        offset = 0
        for depth, width in MATRICES:
            starts.append(offset // LANES)
            offset += depth * width
        self.starts = starts
        self.misc_start = offset // LANES


def fits(mesh):
    return mesh.shape["dp"] == COLUMNS * CORES and mesh.shape["head"] == DEPTH


MESH = pl.DeviceIdType.MESH


class Place:
    def __init__(self):
        dp = lax.axis_index("dp")
        self.z = lax.axis_index("head")
        self.core = dp % CORES
        self.column = dp // CORES
        self.x = self.column % 2
        self.y = self.column // 2
        self.col_x = 2 * self.y + (1 - self.x)
        self.col_y = 2 * (1 - self.y) + self.x
        self.col_d = 2 * (1 - self.y) + (1 - self.x)
        self.peer_x = self.at(self.col_x, self.core, self.z)
        self.peer_y = self.at(self.col_y, self.core, self.z)
        self.peer_d = self.at(self.col_d, self.core, self.z)
        self.peer_core = self.at(self.column, 1 - self.core, self.z)
        self.far = [lax.rem(self.z + d, DEPTH) for d in range(1, DEPTH)]
        self.from_far = [lax.rem(self.z + DEPTH - d, DEPTH) for d in range(1, DEPTH)]
        self.peers_z = [self.at(self.column, self.core, f) for f in self.far]

    def at(self, column, core, z):
        return {"dp": column * CORES + core, "head": z}

    def greet(self):
        barrier = pltpu.get_barrier_semaphore()
        peers = [self.peer_x, self.peer_y, self.peer_d, self.peer_core] + self.peers_z
        for peer in peers:
            pl.semaphore_signal(barrier, inc=1, device_id=peer, device_id_type=MESH)
        pl.semaphore_wait(barrier, len(peers))


def remote(src, dst, send_sem, recv_sem, peer):
    return pltpu.make_async_remote_copy(
        src_ref=src, dst_ref=dst, send_sem=send_sem, recv_sem=recv_sem, device_id=peer,
        device_id_type=MESH,
    )


class Gathering:
    def __init__(self, place, flat, sems):
        self.place = place
        self.flat = flat
        self.sems = sems
        self.sent = []

    def send(self, src, dst, kind, index, peer):
        copy = remote(src, dst, self.sems[kind].at[0, index], self.sems[kind].at[1, index], peer)
        copy.start()
        self.sent.append(copy)

    def got(self, dst, kind, index):
        remote(
            dst, dst, self.sems[kind].at[0, index], self.sems[kind].at[1, index], self.place.peer_x
        ).wait_recv()

    def rows(self, h):
        half = self.flat.shape[-2] // 2
        return slice(h * half, (h + 1) * half)

    def spread(self, own, h):
        p = self.place
        rows = self.rows(h)
        for index, (column, peer) in enumerate(
            ((p.col_x, p.peer_x), (p.col_y, p.peer_y), (p.col_d, p.peer_d))
        ):
            self.send(
                own.at[column, rows], self.flat.at[p.column, p.core, p.z, column, rows], "spread",
                2 * index + h, peer,
            )
        self.flat[p.column, p.core, p.z, p.column, rows] = own[p.column, rows]

    def spread_done(self, h):
        p = self.place
        for index, column in enumerate((p.col_x, p.col_y, p.col_d)):
            self.got(self.flat.at[column, p.core, p.z, p.column, self.rows(h)], "spread", 2 * index + h)

    def along_z(self, k, h):
        p = self.place
        piece = self.flat.at[k, p.core, p.z, p.column, self.rows(h)]
        for d in range(DEPTH - 1):
            self.send(piece, piece, "z", 3 * (2 * k + h) + d, p.peers_z[d])

    def first(self, k, h):
        p = self.place
        n = 2 * k + h
        for d in range(DEPTH - 1):
            self.got(
                self.flat.at[k, p.core, p.from_far[d], p.column, self.rows(h)], "z", 3 * n + d
            )
        piece = self.flat.at[k, p.core, :, p.column, self.rows(h)]
        self.send(piece, piece, "one", 2 * n, p.peer_x)
        self.send(piece, piece, "one", 2 * n + 1, p.peer_y)
        self.send(piece, piece, "core", 5 * n, p.peer_core)

    def second(self, k, h):
        p = self.place
        n = 2 * k + h
        rows = self.rows(h)
        from_x = self.flat.at[k, p.core, :, p.col_x, rows]
        self.got(from_x, "one", 2 * n)
        part = self.flat.at[k, p.core, 0:2, p.col_x, rows]
        self.send(part, part, "two", 2 * n, p.peer_y)
        self.send(from_x, from_x, "core", 5 * n + 1, p.peer_core)
        from_y = self.flat.at[k, p.core, :, p.col_y, rows]
        self.got(from_y, "one", 2 * n + 1)
        part = self.flat.at[k, p.core, 2:4, p.col_y, rows]
        self.send(part, part, "two", 2 * n + 1, p.peer_x)
        self.send(from_y, from_y, "core", 5 * n + 2, p.peer_core)

    def third(self, k, h):
        p = self.place
        n = 2 * k + h
        for side in range(2):
            part = self.flat.at[k, p.core, 2 * side : 2 * side + 2, p.col_d, self.rows(h)]
            self.got(part, "two", 2 * n + side)
            self.send(part, part, "core", 5 * n + 3 + side, p.peer_core)

    def complete(self, k):
        p = self.place
        other = 1 - p.core
        for h in range(2):
            n = 2 * k + h
            rows = self.rows(h)
            for index, column in enumerate((p.column, p.col_x, p.col_y)):
                self.got(self.flat.at[k, other, :, column, rows], "core", 5 * n + index)
            for side in range(2):
                self.got(
                    self.flat.at[k, other, 2 * side : 2 * side + 2, p.col_d, rows], "core",
                    5 * n + 3 + side,
                )

    def finish(self):
        for copy in self.sent:
            copy.wait_send()


GATHER_SEMS = {"spread": 6, "z": 24, "one": 16, "two": 16, "core": 40}


def sem_shapes(counts):
    return [pltpu.SemaphoreType.DMA((2, count)) for count in counts.values()]


def stage_column(plan, flat, staged, k):
    def one(shard, carry):
        core, z = shard // DEPTH, shard % DEPTH
        for quarter in range(COLUMNS):
            base = plan.carry + shard * plan.rows + quarter * plan.quarter
            staged[pl.ds(pl.multiple_of(base, 8), plan.quarter), :] = flat[k, core, z, quarter].astype(F32)
        return carry

    lax.fori_loop(0, CORES * DEPTH, one, 0)


def keep_carry(plan, staged):
    end = plan.carry + plan.per_column
    staged[: plan.carry, :] = staged[end - plan.carry : end, :]


ROW_STEP = 48


def column_rows(plan, k, touching):
    low, high = k * plan.per_column, (k + 1) * plan.per_column
    taken = []
    for index, (depth, width) in enumerate(MATRICES):
        group = 16 * (width // LANES)
        from_low, from_high = low - plan.starts[index], high - plan.starts[index]
        begin = max(0, min(depth, from_low // group * 16))
        if touching:
            end = max(0, min(depth, -(-from_high // group) * 16))
        else:
            end = max(0, min(depth, from_high // group * 16))
        if end > begin:
            taken.append((index, begin, end))
    return taken


def staged_at(plan, k, row):
    return plan.carry + row - k * plan.per_column


def row_loops(rows):
    whole = rows // ROW_STEP
    loops = [(ROW_STEP, 0, whole)] if whole else []
    if rows % ROW_STEP:
        loops.append((16, whole * ROW_STEP, (rows % ROW_STEP) // 16))
    return loops


def form_matrices(plan, staged, matrices, k):
    for index, begin, end in column_rows(plan, k, False):
        blocks = MATRICES[index][1] // LANES
        base = staged_at(plan, k, plan.starts[index] + begin * blocks)
        assert 0 <= base
        target = matrices[index]
        for step_rows, first, count in row_loops(end - begin):

            def one(step, carry, step_rows=step_rows, first=first, blocks=blocks, base=base,
                    begin=begin, target=target):
                row = first + step * step_rows
                for block in range(blocks):
                    got = staged[pl.ds(base + row * blocks + block, step_rows, stride=blocks), :]
                    target[
                        pl.ds(pl.multiple_of(begin + row, 16), step_rows),
                        block * LANES : (block + 1) * LANES,
                    ] = got.astype(BF16)
                return carry

            lax.fori_loop(0, count, one, 0)


def adam_step(params, moment_one, moment_two, grads, flat_index):
    box_part = (flat_index >= 4 * D * D) & (flat_index < 5 * D * D)
    step_rate = jnp.where(box_part, base_rate * layer_decay**12, base_rate * layer_decay)
    decay_mask = jnp.where(flat_index < 5 * D * D + 2 * D * FF, decay_weight, 0.0)
    moment_one = beta_one * moment_one + (1.0 - beta_one) * grads
    moment_two = beta_two * moment_two + (1.0 - beta_two) * grads * grads
    first_hat = moment_one / (1.0 - beta_one**adam_count)
    second_hat = moment_two / (1.0 - beta_two**adam_count)
    update = first_hat / (jnp.sqrt(second_hat) + adam_eps) + decay_mask * params
    return (-step_rate * update, moment_one)


VEC = {}
_at = 0
for _name, _rows in (
    ("q_bias", 6), ("v_bias", 6), ("out_bias", 6), ("gain_one", 6), ("shift_one", 6), ("in_bias", 24),
    ("back_bias", 6), ("gain_two", 6), ("shift_two", 6), ("tables", 9),
):
    VEC[_name] = _at * LANES
    _at += _rows
VEC_ROWS = _at
NOTE_ROWS = 96
NBLOCK = 2 * LANES


def note_place(plan):
    row = plan.misc_start - (CORES * DEPTH * COLUMNS - 1) * plan.rows
    quarter, row = row // plan.quarter, row % plan.quarter
    first = row // 16 * 16
    assert first + NOTE_ROWS <= plan.quarter and row - first + VEC_ROWS <= NOTE_ROWS
    return quarter, first, row - first


def spread_notes(place, own, notes, sems, plan):
    quarter, first, _ = note_place(plan)
    source = own.at[quarter, first : first + NOTE_ROWS]
    home = (place.column == COLUMNS - 1) & (place.core == CORES - 1)
    root = home & (place.z == DEPTH - 1)

    def copy(src, index, peer):
        return remote(src, notes, sems.at[0, index], sems.at[1, 0], peer)

    def arrived():
        copy(notes, 0, place.peer_core).wait_recv()

    @pl.when(root)
    def _():
        notes[...] = own[quarter, first : first + NOTE_ROWS]
        for index, peer in enumerate(place.peers_z):
            copy(source, index, peer).start()

    @pl.when(home & (place.z != DEPTH - 1))
    def _():
        arrived()

    @pl.when(home)
    def _():
        for index, peer in enumerate((place.peer_x, place.peer_y, place.peer_d)):
            copy(notes, 3 + index, peer).start()

    @pl.when((place.core == CORES - 1) & (place.column != COLUMNS - 1))
    def _():
        arrived()

    @pl.when(place.core == CORES - 1)
    def _():
        copy(notes, 6, place.peer_core).start()

    @pl.when(place.core != CORES - 1)
    def _():
        arrived()

    def finish():
        @pl.when(root)
        def _():
            for index, peer in enumerate(place.peers_z):
                copy(source, index, peer).wait_send()

        @pl.when(home)
        def _():
            for index, peer in enumerate((place.peer_x, place.peer_y, place.peer_d)):
                copy(notes, 3 + index, peer).wait_send()

        @pl.when(place.core == CORES - 1)
        def _():
            copy(notes, 6, place.peer_core).wait_send()

    return finish


def turns_table():
    count_freq = D // 8
    freq = np.exp(np.arange(count_freq) * (-math.log(1000.0) / count_freq)) / (2 * math.pi)
    per = np.concatenate([freq, freq])
    phase = np.concatenate([np.zeros(count_freq), np.full(count_freq, 0.25)])
    return np.stack([np.tile(per, 4), np.tile(phase, 4)]).astype(np.float32)


def sin_turns(t):
    t = t - jnp.floor(t + 0.5)
    a = jnp.abs(t)
    m = jnp.minimum(a, 0.5 - a) * (2 * math.pi)
    u = m * m
    poly = -1.0 / 39916800.0
    for term in (1.0 / 362880.0, -1.0 / 5040.0, 1.0 / 120.0, -1.0 / 6.0, 1.0):
        poly = poly * u + term
    s = m * poly
    return jnp.where(t < 0, -s, s)


def token_columns(boxes, lengths, window):
    coords = boxes[window].astype(F32)
    place = lax.broadcasted_iota(jnp.int32, (1, WINLEN), 1)
    doc = jnp.zeros((1, WINLEN), F32)
    anchor = jnp.zeros_like(coords)
    begin = 0
    for d in range(4):
        end = begin + lengths[window, d]
        mine = jnp.where((place >= begin) & (place < end), 1.0, 0.0)
        value = jnp.sum(coords * jnp.where(place == begin, 1.0, 0.0), axis=1, keepdims=True)
        anchor = anchor + value * mine
        doc = doc + mine * float(d)
        begin = end
    anchor = jnp.concatenate([anchor[0:2], anchor[0:2]], axis=0)
    relative = coords - anchor
    centre = jnp.floor((coords[0:2] + coords[2:4]) * 0.5)
    cell = jnp.floor(centre * (1.0 / coord_cell))
    rest = centre - cell * coord_cell
    rows = jnp.concatenate(
        [relative, cell, rest, doc, jnp.zeros((LANES - 9, WINLEN), F32)], axis=0
    )
    return rest, rows.T


def form_features(columns, turns_ref, features):
    lane = lax.broadcasted_iota(jnp.int32, (1, LANES), 1)
    for block in range(D // LANES):
        lanes = slice(block * LANES, (block + 1) * LANES)
        low, high = block * LANES // (D // 4), ((block + 1) * LANES - 1) // (D // 4)
        value = columns[:, low : low + 1]
        if high != low:
            value = jnp.where(
                lane + block * LANES < high * (D // 4), value, columns[:, high : high + 1]
            )
        t = value * turns_ref[0:1, lanes] + turns_ref[1:2, lanes]
        features[:, lanes] = sin_turns(t).astype(BF16)


def form_hots(columns, hot_ref, keyx_ref, keyy_ref, mkey, mquery):
    lane = lax.broadcasted_iota(jnp.int32, (1, LANES), 1)
    part = lane // BUCKETS
    cell = (lane % BUCKETS).astype(F32)
    is_x = jnp.where(columns[:, 4:5] == cell, 1.0, 0.0)
    is_y = jnp.where(columns[:, 5:6] == cell, 1.0, 0.0)
    hot_ref[...] = jnp.where(part % 2 == 0, is_x, is_y).astype(BF16)
    sign = jnp.where(part % 2 == 0, 1.0, -1.0)
    for odd in range(2):
        here = jnp.where(part // 2 == odd, sign, 0.0)
        keyx_ref[odd] = (is_x * here).astype(BF16)
        keyy_ref[odd] = (is_y * here).astype(BF16)
    doc = jnp.where(columns[:, 8:9] == lane.astype(F32), 1.0, 0.0)
    mkey[:, LANES:] = doc.astype(BF16)
    mquery[:, LANES:] = (jnp.where(lane < 4, 1.0 - doc, 0.0) * masked_score).astype(BF16)


def form_tables(tables, bands, tilted):
    row = lax.broadcasted_iota(jnp.int32, (LANES, 1), 0)
    half = BUCKETS // 2
    sub = lax.broadcasted_iota(jnp.int32, (8, LANES), 0)
    sub_wide = lax.broadcasted_iota(jnp.int32, (8, WIDE), 0)
    place = lax.broadcasted_iota(jnp.int32, (1, WIDE), 1)
    wanted = jnp.where(place < 5 * LANES, jnp.clip(place - 2 * LANES, -half, half - 1) + half, 0)
    lane = lax.broadcasted_iota(jnp.int32, (1, LANES), 1)
    turned = jnp.clip(64 - lane, -half, half - 1) + half
    for m in range(4):
        hot_band = jnp.where(row == wanted + m * BUCKETS, 1.0, 0.0).astype(BF16)
        got = matmul(tables, hot_band)
        for n in range(3):
            x = jnp.broadcast_to(got[n : n + 1, :], (8, WIDE))
            for bit in (1, 2, 4):
                x = jnp.where((sub_wide & bit) != 0, pltpu.roll(x, bit, 1), x)
            bands[4 * n + m] = x
        hot_turn = jnp.where(row == turned + m * BUCKETS, 1.0, 0.0).astype(BF16)
        got = matmul(tables, hot_turn)
        for t in (1, 2):
            for n in range(3):
                x = jnp.broadcast_to(got[3 * t + n : 3 * t + n + 1, :], (8, LANES))
                for bit in (1, 2, 4):
                    x = jnp.where((sub & bit) != 0, pltpu.roll(x, bit, 1), x)
                for group in range(BUCKETS // 8):
                    y = x if group == 0 else pltpu.roll(x, 8 * group, 1)
                    tilted[(t - 1) * HEADS + 4 * n + m, 8 * group : 8 * group + 8, :] = y


def pair_rows(tilted, pair):
    lane = lax.broadcasted_iota(jnp.int32, (1, LANES), 1)
    part = lane // BUCKETS
    x0, x1 = tilted[2 * pair], tilted[2 * pair + 1]
    y0, y1 = tilted[HEADS + 2 * pair], tilted[HEADS + 2 * pair + 1]

    def same(value, to):
        return value if to == 64 else pltpu.roll(value, (to - 64) % LANES, 1)

    def less(value, to):
        return pltpu.roll(value, (to - 65) % LANES, 1)

    zero = jnp.zeros_like(x0)
    base_x = jnp.where(part == 0, same(x1, 0), jnp.where(part == 2, same(x0, 64), zero))
    base_y = jnp.where(part == 1, same(y1, 32), jnp.where(part == 3, same(y0, 96), zero))

    def steps(even, odd):
        return jnp.where(
            part < 2,
            jnp.where(part == 0, less(even, 0), same(even, 32)),
            jnp.where(part == 2, less(odd, 64), same(odd, 96)),
        )

    rows = [
        jnp.concatenate([base_x, base_y], axis=0),
        jnp.concatenate([steps(x0, x1), zero], axis=0),
        jnp.concatenate([zero, steps(y0, y1)], axis=0),
    ]
    return jnp.concatenate(rows, axis=1).astype(BF16)


def gelu_and_slope(z):
    a = jnp.abs(z)
    t = 1.0 / (1.0 + (0.3275911 / math.sqrt(2.0)) * a)
    poly = 1.061405429 * 0.5
    for term in (-1.453152027, 1.421413741, -0.284496736, 0.254829592):
        poly = poly * t + 0.5 * term
    e = jnp.exp(-0.5 * z * z)
    tail = poly * t * e
    cdf = jnp.where(z < 0, tail, 1.0 - tail)
    return z * cdf, cdf + z * (e * (1.0 / math.sqrt(2.0 * math.pi)))


def forward_kernel(plan, params_in, hidden_in, cot_in, boxes, lengths, turns, *refs):
    (w_qkv_out, w_out_out, w_in_out, w_back_out, features_out, low_out, q_out, k_out, v_out, probs_out,
     context_out, hat_out, normed_out, vec_out, rstd_out, cot_ref, hot_out, rest_out, share_out) = refs[:19]
    refs = refs[19:]
    (flat, staged, own, w_qkv, w_out, w_box, w_in, w_back, notes, features, hidden, start, start_low, q_ref,
     k_ref, v_ref, hot_ref, key_x, key_y, bands, tilted, wides, scores, context_t, pair_t, hat, narrow,
     square, vec) = refs[:29]
    note_sems, swap_sems, copy_sems, probs_sems = refs[29:33]

    def lend(buffer, slot, lanes):
        return buffer.at[:, slot : slot + lanes]

    less_x, less_y = lend(square, 0, WINLEN), lend(square, WINLEN, WINLEN)
    probs = [lend(square, 2 * WINLEN, WINLEN), lend(square, 3 * WINLEN, WINLEN)]
    kaugs = [lend(narrow, 0, 2 * LANES), lend(narrow, 2 * LANES, 2 * LANES)]
    qaugs = [lend(narrow, 4 * LANES, 2 * LANES), lend(narrow, 6 * LANES, 2 * LANES)]
    met = lend(narrow, 8 * LANES, 3 * LANES)
    place = Place()
    normed_low = hidden
    context = features
    gathering = Gathering(place, flat, dict(zip(GATHER_SEMS, refs[33:])))
    matrices = (w_qkv, w_out, w_box, w_in, w_back)
    written = []

    def write_out(src, dst):
        copy = pltpu.make_async_copy(src, dst, copy_sems.at[len(written)])
        copy.start()
        written.append(copy)

    fetch = pltpu.make_async_copy(params_in, staged.at[: plan.rows], probs_sems.at[0])
    fetch.start()
    place.greet()
    fetch.wait()
    for quarter_at in range(COLUMNS):
        begin = quarter_at * plan.quarter
        own[quarter_at] = staged[begin : begin + plan.quarter, :].astype(BF16)
    gathering.spread(own, 0)
    gathering.spread(own, 1)

    quarter = WINLEN // DEPTH

    def exchange(source, target, kind):
        rows = pl.ds(pl.multiple_of(place.z * quarter, quarter), quarter)
        for d in range(DEPTH - 1):
            gathering_send(source.at[place.far[d]], target.at[rows], kind, d, place.peers_z[d])

    def gathering_send(src, dst, kind, d, peer):
        copy = remote(src, dst, swap_sems.at[kind, 0, d], swap_sems.at[kind, 1, d], peer)
        copy.start()
        gathering.sent.append(copy)

    def exchanged(target, kind):
        for d in range(DEPTH - 1):
            rows = pl.ds(pl.multiple_of(place.from_far[d] * quarter, quarter), quarter)
            remote(
                target.at[rows], target.at[rows], swap_sems.at[kind, 0, d], swap_sems.at[kind, 1, d],
                place.peer_x,
            ).wait_recv()

    finish_notes = spread_notes(place, own, notes, note_sems, plan)
    own_rows = pl.ds(pl.multiple_of(place.z * quarter, quarter), quarter)
    own_hidden = pltpu.make_async_copy(
        hidden_in.at[place.z], hidden.at[own_rows], swap_sems.at[0, 0, DEPTH - 1]
    )
    own_hidden.start()
    own_cot = pltpu.make_async_copy(
        cot_in.at[place.z], cot_ref.at[own_rows], swap_sems.at[1, 0, DEPTH - 1]
    )
    own_cot.start()
    gathering.spread_done(0)
    gathering.along_z(0, 0)
    gathering.spread_done(1)
    gathering.along_z(0, 1)

    rest, columns = token_columns(boxes, lengths, place.z)
    for part in range(BLOCKS):
        rows = slice(part * LANES, (part + 1) * LANES)
        for axis, less in ((0, less_x), (1, less_y)):
            less[rows, :] = jnp.where(
                rest[axis : axis + 1, :] < columns[rows, 6 + axis : 7 + axis], 1.0, 0.0
            ).astype(BF16)
    rest_out[...] = rest
    form_hots(columns, hot_ref, key_x, key_y, kaugs[0], qaugs[0])
    kaugs[1][:, LANES:] = kaugs[0][:, LANES:]
    qaugs[1][:, LANES:] = qaugs[0][:, LANES:]
    hot_out[...] = hot_ref[...]
    gathering.first(0, 0)
    gathering.along_z(1, 0)
    gathering.first(0, 1)
    gathering.along_z(1, 1)
    form_features(columns, turns, features)
    for n in range(D // LANES):
        rows = slice(n * LANES, (n + 1) * LANES)
        context_t[rows, :] = features[:, rows].T
    write_out(context_t, features_out)
    gathering.first(1, 0)
    exchange(hidden_in, hidden, 0)
    gathering.second(0, 0)
    gathering.first(1, 1)
    gathering.second(0, 1)
    _, _, note_row = note_place(plan)
    for row in range(VEC_ROWS):
        at = note_row + row
        vec[0:1, row * LANES : (row + 1) * LANES] = notes[at // 16 * 16 : at // 16 * 16 + 16, :].astype(
            F32
        )[at % 16 : at % 16 + 1, :]
    vec_out[...] = vec[...]
    table_row = note_row + VEC["tables"] // LANES
    assert table_row % 16 == 0
    form_tables(notes[table_row : table_row + 16, :], bands, tilted)

    gathering.third(0, 0)
    gathering.second(1, 0)
    gathering.third(0, 1)
    gathering.second(1, 1)
    gathering.complete(0)
    stage_column(plan, flat, staged, 0)
    exchanged(hidden, 0)
    gathering.along_z(2, 0)
    gathering.along_z(2, 1)
    form_matrices(plan, staged, matrices, 0)
    keep_carry(plan, staged)
    gathering.third(1, 0)
    gathering.third(1, 1)
    gathering.complete(1)
    stage_column(plan, flat, staged, 1)
    form_matrices(plan, staged, matrices, 1)
    keep_carry(plan, staged)
    write_out(w_qkv, w_qkv_out)
    write_out(w_out, w_out_out)

    own_hidden.wait()
    for n in range(D // NBLOCK):
        lanes = slice(n * NBLOCK, (n + 1) * NBLOCK)
        value = hidden[:, lanes].astype(F32) + matmul(features[...], w_box[:, lanes])
        start[:, lanes] = value
        start_low[:, lanes] = value.astype(BF16)
    write_out(start_low, low_out)
    written[0].wait()

    def project(n, carry):
        at = pl.multiple_of(n * NBLOCK, NBLOCK)
        lanes = pl.ds(at, NBLOCK)
        low = start_low[...]
        bias = vec[0:1, pl.ds(pl.multiple_of(VEC["q_bias"] + at, LANES), NBLOCK)]
        got = matmul(low, w_qkv[:, lanes]) + bias
        q_ref[:, lanes] = (got.astype(BF16).astype(F32) * HEAD_DIM ** (-0.5)).astype(BF16)
        k_ref[:, lanes] = matmul(low, w_qkv[:, pl.ds(pl.multiple_of(at + D, LANES), NBLOCK)]).astype(BF16)
        bias = vec[0:1, pl.ds(pl.multiple_of(VEC["v_bias"] + at, LANES), NBLOCK)]
        got = matmul(low, w_qkv[:, pl.ds(pl.multiple_of(at + 2 * D, LANES), NBLOCK)]) + bias
        v_ref[:, lanes] = got.astype(BF16)
        return carry

    lax.fori_loop(0, D // NBLOCK, project, 0)
    write_out(q_ref, q_out)
    write_out(k_ref, k_out)
    write_out(v_ref, v_out)
    gathering.first(2, 0)
    gathering.along_z(3, 0)
    gathering.first(2, 1)
    gathering.along_z(3, 1)

    low, high = half_masks()
    half = 2 * LANES

    def probs_copy(head, odd):
        return pltpu.make_async_copy(probs[odd], probs_out.at[head], probs_sems.at[odd])

    def one_pair(pair, carry):
        at = pl.multiple_of(pair * LANES, LANES)
        lanes = pl.ds(at, LANES)
        values_t = v_ref[:, lanes].T
        met[...] = matmul(hot_ref[:, :64], pair_rows(tilted, pair)).astype(BF16)
        for odd in range(2):
            mine, other = (low, high) if odd == 0 else (high, low)
            kaugs[odd][:, :LANES] = k_ref[:, lanes] * mine + hot_ref[...] * other
            qaugs[odd][:, :LANES] = q_ref[:, lanes] * mine + met[:, :LANES] * other
            skew_groups(bands[2 * pair + odd], wides.at[odd])

            @pl.when(pair > 0)
            def _():
                probs_copy(2 * pair + odd, odd).wait()

        for side in range(2):
            cols = slice(side * half, (side + 1) * half)
            tops = []
            for odd in range(2):
                whole = times_transposed(kaugs[odd][...], qaugs[odd][cols, :])
                steps_x = times_transposed(key_x[odd], met[cols, LANES : 2 * LANES])
                steps_y = times_transposed(key_y[odd], met[cols, 2 * LANES :])
                top = None
                for part in range(BLOCKS):
                    rows = slice(part * LANES, (part + 1) * LANES)
                    bias = []
                    for block in range(2 * side, 2 * side + 2):
                        step = max(-2, min(2, block - part)) + 2
                        bias.append(wides[odd, :, step * LANES : (step + 1) * LANES])
                    s = whole[rows] + jnp.concatenate(bias, axis=1)
                    s = s + steps_x[rows] * less_x[rows, cols].astype(F32)
                    s = s + steps_y[rows] * less_y[rows, cols].astype(F32)
                    scores[odd, rows, :] = s
                    best = jnp.max(s.reshape(LANES // 8, 8, half), axis=0)
                    top = best if top is None else jnp.maximum(top, best)
                tops.append(jnp.max(top, axis=0, keepdims=True))
            for odd in range(2):
                total = None
                for part in range(BLOCKS):
                    rows = slice(part * LANES, (part + 1) * LANES)
                    e = jnp.exp(scores[odd, rows, :] - tops[odd])
                    probs[odd][rows, cols] = e.astype(BF16)
                    add = jnp.sum(e.reshape(LANES // 8, 8, half), axis=0)
                    total = add if total is None else total + add
                share = 1.0 / jnp.sum(total, axis=0, keepdims=True)
                share_out[2 * pair + odd, :, cols] = share
                got = matmul(values_t[odd * HEAD_DIM : (odd + 1) * HEAD_DIM, :], probs[odd][:, cols])
                pair_t[odd * HEAD_DIM : (odd + 1) * HEAD_DIM, cols] = got * share
        for odd in range(2):
            probs_copy(2 * pair + odd, odd).start()
        both = pair_t[...]
        context_t[lanes, :] = both.astype(BF16)
        context[:, lanes] = both.T.astype(BF16)
        return carry

    lax.fori_loop(0, 2, one_pair, 0)
    gathering.second(2, 0)
    gathering.first(3, 0)
    gathering.second(2, 1)
    gathering.first(3, 1)
    exchange(cot_in, cot_ref, 1)
    lax.fori_loop(2, 4, one_pair, 0)
    for h in range(2):
        gathering.third(2, h)
        gathering.second(3, h)
    gathering.complete(2)
    stage_column(plan, flat, staged, 2)
    form_matrices(plan, staged, matrices, 2)
    keep_carry(plan, staged)
    write_out(w_in, w_in_out)
    lax.fori_loop(4, PAIRS, one_pair, 0)
    write_out(context_t, context_out)
    for h in range(2):
        gathering.third(3, h)

    def vector(name):
        return vec[0:1, VEC[name] : VEC[name] + D]

    for n in range(D // NBLOCK):
        lanes = slice(n * NBLOCK, (n + 1) * NBLOCK)
        bias = vec[0:1, VEC["out_bias"] + n * NBLOCK : VEC["out_bias"] + (n + 1) * NBLOCK]
        start[:, lanes] = start[:, lanes] + matmul(context[...], w_out[:, lanes]) + bias

    step_rows = 64

    def norm_first(n, carry):
        rows = pl.ds(pl.multiple_of(n * step_rows, step_rows), step_rows)
        x = start[rows, :]
        centred = x - jnp.mean(x, axis=1, keepdims=True)
        rstd = lax.rsqrt(jnp.mean(centred * centred, axis=1, keepdims=True) + norm_eps)
        xhat = centred * rstd
        hat[rows, :] = xhat
        rstd_out[rows, :] = jnp.broadcast_to(rstd, (step_rows, LANES))
        normed = xhat * vector("gain_one") + vector("shift_one")
        start[rows, :] = normed
        normed_low[rows, :] = normed.astype(BF16)
        return carry

    lax.fori_loop(0, WINLEN // step_rows, norm_first, 0)
    write_out(hat, hat_out)
    write_out(normed_low, normed_out)

    gathering.complete(3)
    stage_column(plan, flat, staged, 3)
    form_matrices(plan, staged, matrices, 3)
    write_out(w_back, w_back_out)
    for odd in range(2):
        probs_copy(0, odd).wait()
    exchanged(cot_ref, 1)
    own_cot.wait()
    for copy in written[1:]:
        copy.wait()
    finish_notes()
    gathering.finish()


def forward_pass(plan, params, hidden_in, cotangent, boxes, lengths):
    anywhere = pl.BlockSpec(memory_space=pl.ANY)
    vmem = pl.BlockSpec(memory_space=pltpu.VMEM)
    token = (WINLEN, D)

    def hbm(shape, dtype=BF16):
        return jax.ShapeDtypeStruct(shape, dtype), anywhere

    def near(shape, dtype=F32):
        return jax.ShapeDtypeStruct(shape, dtype), vmem

    outs = [
        hbm(MATRICES[0]), hbm(MATRICES[1]), hbm(MATRICES[3]), hbm(MATRICES[4]), hbm((D, WINLEN)), hbm(token),
        hbm(token), hbm(token), hbm(token), hbm((HEADS, WINLEN, WINLEN)), hbm((D, WINLEN)),
        hbm(token, F32), hbm(token), near((1, VEC_ROWS * LANES)), near((WINLEN, LANES)),
        near(token, BF16), near((WINLEN, LANES), BF16), near((2, WINLEN)),
        near((HEADS, 1, WINLEN)),
    ]
    scratch = [
        pltpu.VMEM((COLUMNS, CORES, DEPTH, COLUMNS, plan.quarter, LANES), BF16),
        pltpu.VMEM((plan.staged, LANES), F32),
        pltpu.VMEM((COLUMNS, plan.quarter, LANES), BF16),
    ]
    scratch += [pltpu.VMEM(layout, BF16) for layout in MATRICES]
    scratch += [
        pltpu.VMEM((NOTE_ROWS, LANES), BF16),
        pltpu.VMEM(token, BF16),
        pltpu.VMEM(token, BF16),
        pltpu.VMEM(token, F32),
        pltpu.VMEM(token, BF16),
        pltpu.VMEM(token, BF16),
        pltpu.VMEM(token, BF16),
        pltpu.VMEM(token, BF16),
        pltpu.VMEM((WINLEN, LANES), BF16),
        pltpu.VMEM((2, WINLEN, LANES), BF16),
        pltpu.VMEM((2, WINLEN, LANES), BF16),
        pltpu.VMEM((HEADS, 8, WIDE), F32),
        pltpu.VMEM((2 * HEADS, BUCKETS, LANES), F32),
        pltpu.VMEM((2, LANES, 5 * LANES), F32),
        pltpu.VMEM((2, WINLEN, 2 * LANES), F32),
        pltpu.VMEM((D, WINLEN), BF16),
        pltpu.VMEM((LANES, WINLEN), F32),
        pltpu.VMEM(token, F32),
        pltpu.VMEM((WINLEN, 11 * LANES), BF16),
        pltpu.VMEM((WINLEN, 4 * WINLEN), BF16),
        pltpu.VMEM((1, VEC_ROWS * LANES), F32),
        pltpu.SemaphoreType.DMA((2, 7)),
        pltpu.SemaphoreType.DMA((2, 2, DEPTH)),
        pltpu.SemaphoreType.DMA((16,)),
        pltpu.SemaphoreType.DMA((2,)),
    ]
    return pl.pallas_call(
        functools.partial(forward_kernel, plan),
        out_shape=[shape for shape, _ in outs],
        in_specs=[anywhere] * 3 + [vmem, pl.BlockSpec(memory_space=pltpu.SMEM), vmem],
        out_specs=[spec for _, spec in outs],
        scratch_shapes=scratch + sem_shapes(GATHER_SEMS),
        compiler_params=pltpu.CompilerParams(
            collective_id=0, has_side_effects=True, vmem_limit_bytes=62 * 2**20
        ),
        name="forward_pass",
    )(params, hidden_in, cotangent, boxes, lengths, jnp.asarray(turns_table()))


def token_info(doc_lengths, box_coords):
    places = jnp.arange(WINLEN, dtype=jnp.int32)
    first = places == 0
    doc = jnp.zeros((WINLEN,), jnp.int32)
    end = 0
    for d in range(3):
        end = end + doc_lengths[d]
        doc = doc + (places >= end).astype(jnp.int32)
        first = first | (places == end)
    rows = [box_coords[:, c] for c in range(4)] + [doc, first.astype(jnp.int32)]
    return jnp.stack(rows + [jnp.zeros_like(doc)] * 2).astype(F32)


class Reducing:
    def __init__(self, place, flat, swapped, one, two, deep, piece, result, sems, free):
        self.place = place
        self.flat = flat
        self.swapped = swapped
        self.one = one
        self.two = two
        self.deep = deep
        self.piece = piece
        self.result = result
        self.sems = sems
        self.free = free
        self.sent = {k: [] for k in range(COLUMNS)}

    def send(self, k, src, dst, kind, index, peer):
        copy = remote(src, dst, self.sems[kind].at[0, index], self.sems[kind].at[1, index], peer)
        copy.start()
        self.sent[k].append(copy)

    got = Gathering.got

    def settle(self, k):
        for copy in self.sent.pop(k):
            copy.wait_send()

    rows = Gathering.rows

    def swap(self, k, h):
        p = self.place
        slot = k % 2
        if k < 2 and h == 0:
            pl.semaphore_wait(self.free.at[slot], 1)
        self.send(
            k, self.flat.at[slot, 1 - p.core, :, :, self.rows(h)],
            self.swapped.at[slot, :, :, self.rows(h)], "core", 2 * k + h, p.peer_core,
        )

    def first(self, k, h):
        p = self.place
        slot = k % 2
        n, rows = 2 * k + h, self.rows(h)
        self.got(self.swapped.at[slot, :, :, rows], "core", n)

        def one(step, carry):
            z, quarter = step // COLUMNS, step % COLUMNS
            total = self.flat[slot, p.core, z, quarter, rows].astype(F32)
            total = total + self.swapped[slot, z, quarter, rows].astype(F32)
            self.flat[slot, p.core, z, quarter, rows] = total.astype(BF16)
            return carry

        lax.fori_loop(0, DEPTH * COLUMNS, one, 0)
        flat = self.flat
        for side, peer in ((0, p.peer_y), (1, p.peer_x)):
            self.send(
                k, flat.at[slot, p.core, 2 * side : 2 * side + 2, p.col_d, rows],
                self.one.at[k, side, :, rows], "one", 2 * n + side, peer,
            )
        if k >= 2 and h == 1:
            pl.semaphore_signal(
                self.free.at[slot], inc=1, device_id=p.peer_core, device_id_type=MESH
            )

    def second(self, k, h):
        p = self.place
        slot = k % 2
        n, rows = 2 * k + h, self.rows(h)
        for side, column in ((0, p.col_x), (1, p.col_y)):
            self.got(self.one.at[k, side, :, rows], "one", 2 * n + side)

            def one(step, carry, side=side, column=column):
                z = 2 * side + step
                total = self.flat[slot, p.core, z, column, rows].astype(F32)
                total = total + self.one[k, side, step, rows].astype(F32)
                self.flat[slot, p.core, z, column, rows] = total.astype(BF16)
                return carry

            lax.fori_loop(0, 2, one, 0)
        for side, column, peer in ((0, p.col_x, p.peer_x), (1, p.col_y, p.peer_y)):
            self.send(
                k, self.flat.at[slot, p.core, :, column, rows], self.two.at[k, side, :, rows], "two",
                2 * n + side, peer,
            )

    def third(self, k, h):
        p = self.place
        slot = k % 2
        n, rows = 2 * k + h, self.rows(h)
        for side in range(2):
            self.got(self.two.at[k, side, :, rows], "two", 2 * n + side)

        def one(z, carry):
            total = self.flat[slot, p.core, z, p.column, rows].astype(F32)
            total = total + self.two[k, 0, z, rows].astype(F32) + self.two[k, 1, z, rows].astype(F32)
            self.flat[slot, p.core, z, p.column, rows] = total.astype(BF16)
            return carry

        lax.fori_loop(0, DEPTH, one, 0)
        for d in range(DEPTH - 1):
            self.send(
                k, self.flat.at[slot, p.core, p.far[d], p.column, rows], self.deep.at[k, d, rows], "z",
                3 * n + d, p.peers_z[d],
            )

    def fourth(self, k, h):
        p = self.place
        n, rows = 2 * k + h, self.rows(h)
        for d in range(DEPTH - 1):
            self.got(self.deep.at[k, d, rows], "z", 3 * n + d)
        total = self.flat[k % 2, p.core, p.z, p.column, rows].astype(F32)
        for d in range(DEPTH - 1):
            total = total + self.deep[k, d, rows].astype(F32)
        self.piece[k, rows] = total.astype(BF16)

    def giving(self, k, h):
        p = self.place
        sems = self.sems["spread"]
        return remote(
            self.piece.at[k, self.rows(h)], self.result.at[p.column, self.rows(h)],
            sems.at[0, 2 * k + h], sems.at[1, 2 * p.column + h], p.at(k, p.core, p.z),
        )

    def give(self, k, h):
        @pl.when(self.place.column != k)
        def _():
            self.giving(k, h).start()

    def given(self, k, h):
        @pl.when(self.place.column != k)
        def _():
            self.giving(k, h).wait_send()

    def receive(self, out):
        p = self.place
        out[p.column] = self.piece[p.column].astype(F32)
        for column in (p.col_x, p.col_y, p.col_d):
            for h in range(2):
                self.got(self.result.at[column, self.rows(h)], "spread", 2 * column + h)
            out[column] = self.result[column].astype(F32)


REDUCE_SEMS = {"spread": 8, "z": 24, "one": 16, "two": 16, "core": 8}


def unstage_column(plan, flat, staged, k):
    def one(step, carry):
        shard, quarter = step // COLUMNS, step % COLUMNS
        base = plan.carry + shard * plan.rows + quarter * plan.quarter
        piece = staged[pl.ds(pl.multiple_of(base, 8), plan.quarter), :]
        flat[k % 2, shard // DEPTH, shard % DEPTH, quarter] = piece.astype(BF16)
        return carry

    lax.fori_loop(0, CORES * DEPTH * COLUMNS, one, 0)


class Notes:
    def __init__(self, place, notes, slots, sems):
        self.place, self.notes, self.slots, self.sems = place, notes, slots, sems
        p = place
        self.home = (p.column == COLUMNS - 1) & (p.core == CORES - 1)
        self.root = self.home & (p.z == DEPTH - 1)

    def copy(self, slot, peer):
        return remote(
            self.notes, self.slots.at[slot], self.sems.at[0, 0], self.sems.at[1, slot], peer
        )

    def take(self, slot):
        self.copy(slot, self.place.peer_core).wait_recv()
        self.notes[...] = self.notes[...] + self.slots[slot]

    def start(self):
        p = self.place

        @pl.when(p.core != CORES - 1)
        def _():
            self.copy(0, p.peer_core).start()

    def rise(self):
        p = self.place

        @pl.when(p.core == CORES - 1)
        def _():
            self.take(0)

        @pl.when((p.core == CORES - 1) & (p.column != COLUMNS - 1))
        def _():
            self.copy(1 + p.column, p.at(COLUMNS - 1, p.core, p.z)).start()

    def end(self):
        p = self.place

        @pl.when(self.home)
        def _():
            for slot in range(1, 4):
                self.take(slot)

        @pl.when(self.home & (p.z != DEPTH - 1))
        def _():
            self.copy(4 + p.z, p.at(p.column, p.core, DEPTH - 1)).start()

        @pl.when(self.root)
        def _():
            for slot in range(4, 7):
                self.take(slot)

        @pl.when(jnp.logical_not(self.root))
        def _():
            self.copy(0, p.peer_core).wait_send()


def cell_sums(whole, less):
    lane = lax.broadcasted_iota(jnp.int32, (1, LANES), 1)
    sub = lax.broadcasted_iota(jnp.int32, (8, LANES), 0)
    sums = []
    for axis in range(2):
        rows = slice(axis * BUCKETS, (axis + 1) * BUCKETS)
        every = pltpu.roll(whole[rows], (BUCKETS - axis * BUCKETS) % LANES, 1)
        below = pltpu.roll(less[rows], (BUCKETS - axis * BUCKETS) % LANES, 1)
        inside = (lane >= BUCKETS) & (lane < 2 * BUCKETS)
        every = jnp.where(inside, every, 0.0)
        below = jnp.where(inside, below, 0.0)
        x = every - below + pltpu.roll(below, LANES - 1, 1)
        total = None
        for group in range(BUCKETS // 8):
            y = x[8 * group : 8 * group + 8]
            y = y if group == 0 else pltpu.roll(y, LANES - 8 * group, 1)
            total = y if total is None else total + y
        for bit in (1, 2, 4):
            total = jnp.where((sub & bit) != 0, pltpu.roll(total, LANES - bit, 1), total)
        sums.append(jnp.sum(total, axis=0, keepdims=True))
    return sums


def exact_dot(a, b):
    return jnp.dot(a, b, preferred_element_type=F32, precision=lax.Precision.HIGHEST)


def bucket_rows(cell_ref, diag_ref):
    half = BUCKETS // 2
    column = lax.broadcasted_iota(jnp.int32, (1, LANES), 1)
    row = lax.broadcasted_iota(jnp.int32, (LANES, 1), 0)
    to = jnp.clip(row - BUCKETS, -half, half - 1) + half
    place = lax.broadcasted_iota(jnp.int32, (WIDE, 1), 0)
    along = place - LANES
    far = jnp.where(place < LANES, 0, jnp.where(place < 5 * LANES, 0, BUCKETS - 1))
    along = jnp.where(
        (place >= LANES) & (place < 4 * LANES),
        jnp.clip(along - LANES, -half, half - 1) + half,
        far,
    )
    first, rest = None, None
    zero = jnp.zeros((5, WIDE), F32)
    for m in range(4):
        hot_along = jnp.where(along + m * BUCKETS == column, 1.0, 0.0)
        got = exact_dot(
            jnp.concatenate([diag_ref[4 * n + m] for n in range(3)] + [zero], axis=0), hot_along
        )
        first = got if first is None else first + got
        hot_cell = jnp.where(to + m * BUCKETS == column, 1.0, 0.0)
        rows = [cell_ref[t * HEADS + 4 * n + m] for t in range(2) for n in range(3)]
        got = exact_dot(jnp.concatenate(rows + [zero[:2, :LANES]], axis=0), hot_cell)
        rest = got if rest is None else rest + got
    return jnp.concatenate([first[:3], rest[:6]], axis=0)


def backward_kernel(
    plan, w_back_in, w_in_in, w_out_in, w_qkv_in, normed_in, low_in, features_in,
    context_in, q_in, k_in, v_in, probs_in, hat_in, cot_in, rstd_ref, vec, hot_ref, rest_ref, share_ref,
    *refs,
):
    out, output_pos, hidden_pos, spill = refs[:4]
    (flat, staged, swapped, one_buf, two_buf, deep, piece, result, active, slope, w_back, w_in, w_out,
     turned, context_t, q_ref, k_ref, v_ref, hat, second, branch, dctx, probs, less_x,
     less_y, scores_odd, bands, hot_t, pair_t, scaled, share_cols, vecg, cell_rows, diag_rows, notes, slots,
     ) = refs[4:40]
    load_sems, probs_sems, free, pos_sems, note_sems, spill_sems = refs[40:46]
    place = Place()
    reducing = Reducing(
        place, flat, swapped, one_buf, two_buf, deep, piece, result,
        dict(zip(REDUCE_SEMS, refs[46:])), free,
    )
    climbing = Notes(place, notes, slots, note_sems)
    loads = {}

    def load(name, src, dst):
        loads[name] = pltpu.make_async_copy(src, dst, load_sems.at[len(loads)])
        loads[name].start()

    mixed = active.at[:, : 3 * D]
    grad_attn = branch
    w_qkv = w_in.at[:, : 3 * D]
    hidden_low = dctx
    features_t = w_back.at[:D, :WINLEN]
    low_t = w_out.at[:WINLEN]
    scores = [hat.at[:, :WINLEN], scores_odd]
    dscores = [slope.at[:, :WINLEN], slope.at[:, WINLEN : 2 * WINLEN]]
    output_low = w_out.at[:WINLEN]
    output_low = w_out.at[:WINLEN]
    dscores_x = [slope.at[:, 2 * WINLEN : 3 * WINLEN], slope.at[:, 3 * WINLEN : 4 * WINLEN]]
    dscores_y = [slope.at[:, 4 * WINLEN : 5 * WINLEN], slope.at[:, 5 * WINLEN :]]

    load("normed", normed_in, dctx)
    load("w_in", w_in_in, w_in)
    load("hat", hat_in, hat)
    load("w_back", w_back_in, w_back)
    load("cot", cot_in, branch)

    at = staged_at(plan, COLUMNS - 1, plan.misc_start)
    staged[at:, :] = jnp.zeros((plan.staged - at, LANES), F32)
    place.greet()

    quarter = WINLEN // DEPTH
    positions = []

    def to_pos(source, target, kind):
        for d in range(DEPTH - 1):
            rows = pl.ds(pl.multiple_of(place.far[d] * quarter, quarter), quarter)
            copy = remote(
                source.at[rows], target.at[place.z], pos_sems.at[kind, 0, d], pos_sems.at[kind, 1, d],
                place.peers_z[d],
            )
            copy.start()
            positions.append(copy)
        rows = pl.ds(pl.multiple_of(place.z * quarter, quarter), quarter)
        copy = pltpu.make_async_copy(
            source.at[rows], target.at[place.z], pos_sems.at[kind, 0, DEPTH - 1]
        )
        copy.start()
        return copy

    def in_pos(target, kind):
        for d in range(DEPTH - 1):
            there = target.at[place.from_far[d]]
            remote(
                there, there, pos_sems.at[kind, 0, d], pos_sems.at[kind, 1, d], place.peer_x
            ).wait_recv()


    def store(k, index, row, value, first_block=0):
        blocks = MATRICES[index][1] // LANES
        base = staged_at(plan, k, plan.starts[index]) + row * blocks + first_block
        for block in range(value.shape[1] // LANES):
            staged[pl.ds(base + block, value.shape[0], stride=blocks), :] = value[
                :, block * LANES : (block + 1) * LANES
            ]

    def column_sum(value):
        return jnp.sum(value, axis=0, keepdims=True)

    def keep_vector(name, lanes_at, value):
        at = pl.multiple_of(VEC[name] + lanes_at, LANES)
        vecg[0:1, pl.ds(at, value.shape[1])] = value

    def vector(name, at=0, size=D):
        return vec[0:1, pl.ds(pl.multiple_of(VEC[name] + at, LANES), size)]

    loads["normed"].wait()
    loads["w_in"].wait()

    def widen(n, carry):
        at = pl.multiple_of(n * NBLOCK, NBLOCK)
        lanes = pl.ds(at, NBLOCK)
        inner_act = matmul(dctx[...], w_in[:, lanes]) + vector("in_bias", at, NBLOCK)
        value, change = gelu_and_slope(inner_act)
        active[:, lanes] = value.astype(BF16)
        slope[:, lanes] = change.astype(BF16)
        return carry

    lax.fori_loop(0, FF // NBLOCK, widen, 0, unroll=2)
    loads["hat"].wait()
    loads["w_back"].wait()
    for n in range(D // NBLOCK):
        lanes = slice(n * NBLOCK, (n + 1) * NBLOCK)
        normed = hat[:, lanes] * vector("gain_one", n * NBLOCK, NBLOCK) + vector(
            "shift_one", n * NBLOCK, NBLOCK
        )
        second[:, lanes] = (
            normed + matmul(active[...], w_back[:, lanes]) + vector("back_bias", n * NBLOCK, NBLOCK)
        )
    loads["cot"].wait()
    step_rows = 64
    for name in ("gain_two", "shift_two", "back_bias", "gain_one", "shift_one", "out_bias"):
        keep_vector(name, 0, jnp.zeros((1, D), F32))

    def add_vector(name, term):
        lanes = slice(VEC[name], VEC[name] + D)
        vecg[0:1, lanes] = vecg[0:1, lanes] + column_sum(term)

    def norm_second(n, carry):
        rows = pl.ds(pl.multiple_of(n * step_rows, step_rows), step_rows)
        x = second[rows, :]
        centred = x - jnp.mean(x, axis=1, keepdims=True)
        rstd = lax.rsqrt(jnp.mean(centred * centred, axis=1, keepdims=True) + norm_eps)
        xhat = centred * rstd
        gain = vector("gain_two")
        output_low[rows, :] = (xhat * gain + vector("shift_two")).astype(BF16)
        cot = branch[rows, :].astype(F32)
        prod = cot * xhat
        gc = cot * gain
        mean_one = jnp.mean(gc, axis=1, keepdims=True)
        mean_two = jnp.mean(prod * gain, axis=1, keepdims=True)
        value = rstd * (gc - mean_one - xhat * mean_two)
        second[rows, :] = value
        value = value.astype(BF16)
        branch[rows, :] = value
        add_vector("gain_two", prod)
        add_vector("shift_two", cot)
        add_vector("back_bias", value.astype(F32))
        return carry

    lax.fori_loop(0, WINLEN // step_rows, norm_second, 0, unroll=2)
    own_output = to_pos(output_low, output_pos, 0)

    def back_rows(k, size, begin, count):
        def body(n, carry):
            row = pl.multiple_of(begin + n * size, LANES)
            turned[:size, :] = active[:, pl.ds(row, size)].T
            store(k, 4, row, matmul(turned[:size, :], branch[...]))
            return carry

        lax.fori_loop(0, count, body, 0)

    back_rows(3, WINLEN, 512, FF // WINLEN - 1)
    unstage_column(plan, flat, staged, 3)
    reducing.swap(3, 0)
    reducing.swap(3, 1)

    back_rows(2, WINLEN, 0, 1)
    back_rows(2, LANES, 512, 1)

    def inner(n, carry):
        at = pl.multiple_of(n * NBLOCK, NBLOCK)
        lanes = pl.ds(at, NBLOCK)
        value = times_transposed(branch[...], w_back[lanes, :]) * slope[:, lanes].astype(F32)
        value = value.astype(BF16)
        slope[:, lanes] = value
        keep_vector("in_bias", at, column_sum(value.astype(F32)))
        return carry

    lax.fori_loop(0, FF // NBLOCK, inner, 0, unroll=2)
    grad_inner = slope
    reducing.first(3, 0)
    reducing.first(3, 1)

    for n in range(D // NBLOCK):
        rows = slice(n * NBLOCK, (n + 1) * NBLOCK)
        turned[rows, :] = dctx[:, rows].T

    def in_rows(k, begin, end):
        def body(n, carry):
            lanes = pl.ds(pl.multiple_of(n * NBLOCK, NBLOCK), NBLOCK)
            got = matmul(turned[begin:end, :], grad_inner[:, lanes])
            store(k, 3, begin, got, n * (NBLOCK // LANES))
            return carry

        lax.fori_loop(0, FF // NBLOCK, body, 0)

    in_rows(2, 288, D)
    unstage_column(plan, flat, staged, 2)
    reducing.swap(2, 0)
    reducing.swap(2, 1)
    reducing.second(3, 0)
    reducing.second(3, 1)

    load("context", context_in, context_t)
    load("q", q_in, q_ref)
    load("k", k_in, k_ref)
    load("v", v_in, v_ref)
    for odd in range(2):
        pltpu.make_async_copy(probs_in.at[odd], probs.at[odd], probs_sems.at[odd]).start()
    for n in range(D // NBLOCK):
        lanes = slice(n * NBLOCK, (n + 1) * NBLOCK)
        second[:, lanes] = second[:, lanes] + times_transposed(grad_inner[...], w_in[lanes, :])
    load("w_qkv", w_qkv_in, w_qkv)
    load("features", features_in, features_t)
    reducing.first(2, 0)
    reducing.first(2, 1)

    for copy in positions:
        copy.wait_send()
    own_output.wait()
    load("w_out", w_out_in, w_out)

    def norm_first(n, carry):
        rows = pl.ds(pl.multiple_of(n * step_rows, step_rows), step_rows)
        grad = second[rows, :]
        xhat = hat[rows, :]
        prod = grad * xhat
        gain = vec[0:1, VEC["gain_one"] : VEC["gain_one"] + D]
        gc = grad * gain
        mean_one = jnp.mean(gc, axis=1, keepdims=True)
        mean_two = jnp.mean(prod * gain, axis=1, keepdims=True)
        value = rstd_ref[rows, 0:1] * (gc - mean_one - xhat * mean_two)
        second[rows, :] = value
        value = value.astype(BF16)
        grad_attn[rows, :] = value
        add_vector("gain_one", prod)
        add_vector("shift_one", grad)
        add_vector("out_bias", value.astype(F32))
        return carry

    lax.fori_loop(0, WINLEN // step_rows, norm_first, 0, unroll=2)
    reducing.third(3, 0)
    reducing.third(3, 1)
    loads["w_out"].wait()
    for n in range(D // NBLOCK):
        lanes = slice(n * NBLOCK, (n + 1) * NBLOCK)
        dctx[:, lanes] = times_transposed(grad_attn[...], w_out[lanes, :]).astype(BF16)
    load("low", low_in, low_t)
    loads["context"].wait()
    in_rows(1, 0, 304)
    reducing.second(2, 0)
    reducing.second(2, 1)

    def out_rows(k, begin, end):
        for n in range(D // NBLOCK):
            lanes = slice(n * NBLOCK, (n + 1) * NBLOCK)
            got = matmul(context_t[begin:end, :], grad_attn[:, lanes])
            store(k, 1, begin, got, n * (NBLOCK // LANES))

    out_rows(1, 192, D)
    reducing.fourth(3, 0)
    reducing.fourth(3, 1)
    reducing.give(3, 0)
    reducing.give(3, 1)

    low, high = half_masks()
    rest = rest_ref[...]
    columns = jnp.concatenate([rest, jnp.zeros((LANES - 2, WINLEN), F32)], axis=0).T
    for part in range(BLOCKS):
        rows = slice(part * LANES, (part + 1) * LANES)
        for axis, less in ((0, less_x), (1, less_y)):
            less[rows, :] = jnp.where(
                rest[axis : axis + 1, :] < columns[rows, axis : axis + 1], 1.0, 0.0
            ).astype(BF16)
    hot_t[...] = hot_ref[...].T
    lane = lax.broadcasted_iota(jnp.int32, (1, LANES), 1)
    scale = HEAD_DIM ** (-0.5)
    of_x = jnp.where((lane // BUCKETS) % 2 == 0, 1.0, 0.0)
    share_cols[...] = jnp.concatenate(
        [share_ref[head] for head in range(HEADS)] + [jnp.zeros((LANES - HEADS, WINLEN), F32)], axis=0
    ).T
    for name in ("q", "k", "v"):
        loads[name].wait()

    def probs_copy(head, odd):
        return pltpu.make_async_copy(probs_in.at[head], probs.at[odd], probs_sems.at[odd])

    def spill_copy(head, odd):
        return pltpu.make_async_copy(dscores[odd], spill.at[head], spill_sems.at[odd])

    def one_pair(pair, carry):
        at = pl.multiple_of(pair * LANES, LANES)
        lanes = pl.ds(at, LANES)
        keys_t = k_ref[:, lanes].T
        both = pltpu.roll(share_cols[...], lax.rem(LANES - 2 * pair, LANES), 1)
        both = jnp.where(lane < HEAD_DIM, both[:, 0:1], both[:, 1:2])
        scaled[...] = (dctx[:, lanes].astype(F32) * both).astype(BF16)
        grad_context = dctx[:, lanes]
        dots = []
        for odd in range(2):
            mine, other = (low, high) if odd == 0 else (high, low)
            head = 2 * pair + odd
            probs_copy(head, odd).wait()
            products = times_transposed(v_ref[:, lanes] * mine, grad_context)
            dot = None
            for part in range(BLOCKS):
                rows = slice(part * LANES, (part + 1) * LANES)
                dp = products[rows]
                scores[odd][rows, :] = dp
                add = dp * probs[odd, rows, :].astype(F32)
                add = jnp.sum(add.reshape(LANES // 8, 8, WINLEN), axis=0)
                dot = add if dot is None else dot + add
            dots.append(column_sum(dot) * share_ref[head])
        for odd in range(2):
            head = 2 * pair + odd
            share = share_ref[head]

            @pl.when(pair > 0)
            def _():
                spill_copy(head, odd).wait()

            for part in range(BLOCKS):
                rows = slice(part * LANES, (part + 1) * LANES)
                ds = probs[odd, rows, :].astype(F32) * ((scores[odd][rows, :] - dots[odd]) * share)
                dscores[odd][rows, :] = ds.astype(BF16)
            spill_copy(head, odd).start()
        for odd in range(2):
            head = 2 * pair + odd
            keys_grad = matmul(dscores[odd][...], q_ref[:, lanes])
            values_grad = matmul(probs[odd], scaled[...])

            pair_t[odd * HEAD_DIM : (odd + 1) * HEAD_DIM, :] = matmul(
                keys_t[odd * HEAD_DIM : (odd + 1) * HEAD_DIM, :], dscores[odd][...]
            )
            for which, value in ((1, keys_grad), (2, values_grad)):
                there = pl.ds(pl.multiple_of(at + which * D, LANES), LANES)
                value = value.astype(BF16)
                if odd:
                    value = mixed[:, there] * low + value * high
                mixed[:, there] = value

        @pl.when(pair < PAIRS - 1)
        def _():
            for odd in range(2):
                probs_copy(2 * pair + odd + 2, odd).start()

        value = (pair_t[...].T * scale).astype(BF16)
        mixed[:, lanes] = value
        keep_vector("q_bias", at, column_sum(value.astype(F32)))
        there = pl.ds(pl.multiple_of(at + 2 * D, LANES), LANES)
        keep_vector("v_bias", at, column_sum(mixed[:, there].astype(F32)))
        return carry

    lax.fori_loop(0, 2, one_pair, 0)
    reducing.third(2, 0)
    reducing.third(2, 1)
    lax.fori_loop(2, 4, one_pair, 0)
    reducing.fourth(2, 0)
    reducing.fourth(2, 1)
    reducing.give(2, 0)
    reducing.give(2, 1)
    lax.fori_loop(4, PAIRS, one_pair, 0)

    for odd in range(2):
        spill_copy(0, odd).wait()
    loads["w_qkv"].wait()
    for n in range(D // NBLOCK):
        lanes = slice(n * NBLOCK, (n + 1) * NBLOCK)
        value = second[:, lanes] + times_transposed(mixed[...], w_qkv[lanes, :])
        hidden_low[:, lanes] = value.astype(BF16)
    own_hidden = to_pos(hidden_low, hidden_pos, 1)
    loads["features"].wait()
    for n in range(D // NBLOCK):
        lanes = slice(n * NBLOCK, (n + 1) * NBLOCK)
        store(1, 2, 0, matmul(features_t[...], hidden_low[:, lanes]), n * (NBLOCK // LANES))
    reducing.settle(3)
    unstage_column(plan, flat, staged, 1)
    reducing.swap(1, 0)
    reducing.swap(1, 1)

    loads["low"].wait()
    for n in range(D // NBLOCK):
        rows = slice(n * NBLOCK, (n + 1) * NBLOCK)
        turned[rows, :] = low_t[:, rows].T

    def qkv_rows(n, carry):
        lanes = pl.ds(pl.multiple_of(n * NBLOCK, NBLOCK), NBLOCK)
        store(0, 0, 0, matmul(turned[...], mixed[:, lanes]), n * (NBLOCK // LANES))
        return carry

    lax.fori_loop(0, 3 * D // NBLOCK, qkv_rows, 0)
    out_rows(0, 0, 208)
    reducing.settle(2)
    unstage_column(plan, flat, staged, 0)
    reducing.swap(0, 0)
    reducing.swap(0, 1)

    def fetch_scores(head):
        there = slope.at[:, pl.ds(pl.multiple_of(lax.rem(head, 2) * WINLEN, WINLEN), WINLEN)]
        return pltpu.make_async_copy(spill.at[head], there, spill_sems.at[lax.rem(head, 2)])

    cells = [hot_ref[...] * of_x.astype(BF16), hot_ref[...] * (1.0 - of_x).astype(BF16)]
    band = bands.at[0]
    parts_x = slope.at[:, 2 * WINLEN : 3 * WINLEN]
    parts_y = slope.at[:, 3 * WINLEN : 4 * WINLEN]

    def one_table(head, carry):
        fetch_scores(head).wait()

        @pl.when(head < HEADS - 1)
        def _():
            fetch_scores(head + 1).start()

        here = slope.at[:, pl.ds(pl.multiple_of(lax.rem(head, 2) * WINLEN, WINLEN), WINLEN)]
        band[...] = jnp.zeros_like(band)
        for part in range(BLOCKS):
            rows = slice(part * LANES, (part + 1) * LANES)
            low_ds = here[rows, :]
            parts_x[rows, :] = low_ds * less_x[rows, :]
            parts_y[rows, :] = low_ds * less_y[rows, :]
            ds = low_ds.astype(F32)
            for block in range(BLOCKS):
                step = max(-2, min(2, block - part)) + 2
                where = slice(step * LANES, (step + 1) * LANES)
                band[:, where] = band[:, where] + ds[:, block * LANES : (block + 1) * LANES]
        whole = matmul(here[...], hot_ref[...])
        less = matmul(parts_x[...], cells[0]) + matmul(parts_y[...], cells[1])
        diag_rows[head, :, LANES : 5 * LANES] = diagonal_sums(band)
        diag_rows[head, :, :LANES] = column_sum(band[:, :LANES])
        diag_rows[head, :, 5 * LANES :] = column_sum(band[:, 4 * LANES :])
        sums = []
        for summed in (whole, less):
            first = summed.astype(BF16)
            remainder = (summed - first.astype(F32)).astype(BF16)
            sums.append(matmul(hot_t[:64, :], first) + matmul(hot_t[:64, :], remainder))
        for axis, value in enumerate(cell_sums(sums[0], sums[1])):
            cell_rows[axis * HEADS + head] = value
        return carry

    fetch_scores(0).start()
    reducing.first(1, 0)
    reducing.first(1, 1)
    lax.fori_loop(0, 4, one_table, 0)
    reducing.first(0, 0)
    reducing.second(1, 0)
    reducing.first(0, 1)
    reducing.second(1, 1)
    lax.fori_loop(4, 8, one_table, 0)
    reducing.second(0, 0)
    reducing.third(1, 0)
    reducing.second(0, 1)
    reducing.third(1, 1)
    lax.fori_loop(8, HEADS, one_table, 0)
    notes[...] = jnp.zeros_like(notes)
    table = VEC["tables"] // LANES
    for row in range(table):
        notes[row : row + 1, :] = vecg[0:1, row * LANES : (row + 1) * LANES]
    notes[table : table + 9, :] = bucket_rows(cell_rows, diag_rows)
    climbing.start()
    reducing.third(0, 0)
    reducing.fourth(1, 0)
    reducing.give(1, 0)
    climbing.rise()
    reducing.third(0, 1)
    reducing.fourth(1, 1)
    reducing.give(1, 1)
    reducing.fourth(0, 0)
    reducing.give(0, 0)
    climbing.end()
    reducing.fourth(0, 1)
    reducing.give(0, 1)
    reducing.receive(out)
    note_quarter, note_first, note_row = note_place(plan)
    base = note_first + note_row

    @pl.when(climbing.root)
    def _():
        out[note_quarter, base : base + MISC_ROWS, :] = (
            out[note_quarter, base : base + MISC_ROWS, :] + notes[:MISC_ROWS, :]
        )

    in_pos(output_pos, 0)
    in_pos(hidden_pos, 1)
    own_hidden.wait()
    for copy in positions[DEPTH - 1 :]:
        copy.wait_send()
    for k in range(COLUMNS):
        for h in range(2):
            reducing.given(k, h)
    reducing.settle(1)
    reducing.settle(0)


def backward_pass(plan, operands):
    anywhere = pl.BlockSpec(memory_space=pl.ANY)
    vmem = pl.BlockSpec(memory_space=pltpu.VMEM)
    token = (WINLEN, D)
    block = (plan.quarter, LANES)
    positions = jax.ShapeDtypeStruct((DEPTH, WINLEN // DEPTH, D), BF16)
    scratch = [
        pltpu.VMEM((2, CORES, DEPTH, COLUMNS) + block, BF16),
        pltpu.VMEM((plan.staged, LANES), F32),
        pltpu.VMEM((2, DEPTH, COLUMNS) + block, BF16),
        pltpu.VMEM((COLUMNS, 2, 2) + block, BF16),
        pltpu.VMEM((COLUMNS, 2, DEPTH) + block, BF16),
        pltpu.VMEM((COLUMNS, DEPTH - 1) + block, BF16),
        pltpu.VMEM((COLUMNS,) + block, BF16),
        pltpu.VMEM((COLUMNS,) + block, BF16),
        pltpu.VMEM((WINLEN, FF), BF16),
        pltpu.VMEM((WINLEN, FF), BF16),
        pltpu.VMEM((FF, D), BF16),
        pltpu.VMEM((D, FF), BF16),
        pltpu.VMEM((D, D), BF16),
        pltpu.VMEM((D, WINLEN), BF16),
        pltpu.VMEM((D, WINLEN), BF16),
        pltpu.VMEM(token, BF16),
        pltpu.VMEM(token, BF16),
        pltpu.VMEM(token, BF16),
        pltpu.VMEM(token, F32),
        pltpu.VMEM(token, F32),
        pltpu.VMEM(token, BF16),
        pltpu.VMEM(token, BF16),
        pltpu.VMEM((2, WINLEN, WINLEN), BF16),
        pltpu.VMEM((WINLEN, WINLEN), BF16),
        pltpu.VMEM((WINLEN, WINLEN), BF16),
        pltpu.VMEM((WINLEN, WINLEN), F32),
        pltpu.VMEM((1, LANES, 5 * LANES), F32),
        pltpu.VMEM((LANES, WINLEN), BF16),
        pltpu.VMEM((LANES, WINLEN), F32),
        pltpu.VMEM((WINLEN, LANES), BF16),
        pltpu.VMEM((WINLEN, LANES), F32),
        pltpu.VMEM((1, VEC_ROWS * LANES), F32),
        pltpu.VMEM((2 * HEADS, 1, LANES), F32),
        pltpu.VMEM((HEADS, 1, WIDE), F32),
        pltpu.VMEM((NOTE_ROWS, LANES), F32),
        pltpu.VMEM((7, NOTE_ROWS, LANES), F32),
        pltpu.SemaphoreType.DMA((16,)),
        pltpu.SemaphoreType.DMA((2,)),
        pltpu.SemaphoreType.REGULAR((2,)),
        pltpu.SemaphoreType.DMA((2, 2, DEPTH)),
        pltpu.SemaphoreType.DMA((2, 7)),
        pltpu.SemaphoreType.DMA((2,)),
    ]
    return pl.pallas_call(
        functools.partial(backward_kernel, plan),
        out_shape=[
            jax.ShapeDtypeStruct((COLUMNS,) + block, F32), positions, positions,
            jax.ShapeDtypeStruct((HEADS, WINLEN, WINLEN), BF16),
        ],
        in_specs=[anywhere] * 14 + [vmem] * 5,
        out_specs=[vmem] + [anywhere] * 3,
        scratch_shapes=scratch + sem_shapes(REDUCE_SEMS),
        compiler_params=pltpu.CompilerParams(
            collective_id=1, has_side_effects=True, vmem_limit_bytes=62 * 2**20
        ),
        name="backward_pass",
    )(*operands)


def fast_shards(hidden_in, cotangent, box_coords, doc_lengths, params, moment_one, moment_two):
    shard_len = params.shape[0]
    plan = Plan(shard_len)
    (proj_qkv, proj_out, proj_in, proj_back, features_t, start_low, queries, keys, values, probs, context_t,
     xhat, normed_low, vec, rstd, cot, hot_two,
     rest_rows, share) = forward_pass(
        plan, params.reshape(plan.rows, LANES), hidden_in, cotangent,
        jnp.transpose(box_coords, (0, 2, 1)), doc_lengths,
    )
    summed, output_low, grad_hidden, _ = backward_pass(
        Plan(shard_len, carry=5 * LANES),
        (proj_back, proj_in, proj_out, proj_qkv, normed_low, start_low, features_t, context_t, queries, keys,
         values, probs, xhat, cot, rstd, vec, hot_two, rest_rows, share),
    )
    grad_share = summed.reshape(plan.padded, LANES)[: plan.rows].reshape(-1)
    return finish_step(output_low, grad_hidden, grad_share, params, moment_one, moment_two)


def finish_step(output_low, grad_hidden, grad_share, params, moment_one, moment_two):
    shard_len = params.shape[0]
    index = lax.axis_index("dp") * lax.axis_size("head") + lax.axis_index("head")
    flat_index = index * shard_len + jnp.arange(shard_len, dtype=jnp.int32)
    param_step, new_one = adam_step(params, moment_one, moment_two, grad_share, flat_index)
    return (output_low, grad_hidden, grad_share, param_step, new_one)


def to_windows(shard):
    return lax.all_to_all(shard, "head", split_axis=0, concat_axis=1, tiled=True)


def to_positions(window):
    return lax.all_to_all(window, "head", split_axis=1, concat_axis=0, tiled=True)


def plain_shards(hidden_in, cotangent, box_coords, doc_lengths, params, moment_one, moment_two):
    head_pos = lax.axis_index("head")
    groups = lax.axis_size("head")
    shard_len = params.shape[0]
    flat_params = lax.all_gather(params.astype(BF16), ("dp", "head"), axis=0, tiled=True)
    pieces = unpack(flat_params)
    hidden = to_windows(hidden_in).reshape(WINLEN, D)
    cot = to_windows(cotangent).reshape(WINLEN, D)
    own_box = lax.dynamic_index_in_dim(box_coords, head_pos, 0, keepdims=False)
    own_lengths = lax.dynamic_index_in_dim(doc_lengths, head_pos, 0, keepdims=False)
    chosen, relative, centre_x, centre_y = window_layout(own_lengths, own_box)
    features = box_features(relative).astype(BF16)

    proj_qkv, proj_out, proj_box, proj_in, proj_back = pieces[:5]
    qv_bias, out_bias, norm_one, in_bias, back_bias, norm_two, tables = pieces[5:]
    ops = bias_operands(tables, chosen, centre_x, centre_y)
    start_state = hidden.astype(F32) + matmul(features, proj_box)
    start_low = start_state.astype(BF16)
    qv_float = qv_bias.astype(F32)
    mixed = matmul(start_low, proj_qkv)
    queries = (mixed[:, :D] + qv_float[0]).astype(BF16) * jnp.asarray(HEAD_DIM ** (-0.5), BF16)
    keys = mixed[:, D : 2 * D].astype(BF16)
    values = (mixed[:, 2 * D :] + qv_float[1]).astype(BF16)

    probs, context_t = attention_forward(queries, keys, values, ops)
    first_sum = start_state + rows_inner(context_t, proj_out) + out_bias.astype(F32)
    normed, norm_one_back = jax.vjp(layer_norm, first_sum, norm_one.astype(F32))
    normed_low = normed.astype(BF16)
    inner_act = matmul(normed_low, proj_in) + in_bias.astype(F32)
    active, gelu_back = jax.vjp(gelu_exact, inner_act)
    active_low = active.astype(BF16)
    second_sum = normed + matmul(active_low, proj_back) + back_bias.astype(F32)
    output, norm_two_back = jax.vjp(layer_norm, second_sum, norm_two.astype(F32))
    output_low = to_positions(output.astype(BF16).reshape(1, WINLEN, D))

    grad_second, grad_norm_two = norm_two_back(cot.astype(F32))
    grad_branch = grad_second.astype(BF16)
    grad_proj_back = rows_inner(active_low, grad_branch)
    grad_back_bias = jnp.sum(grad_branch.astype(F32), axis=0)
    (grad_inner_f,) = gelu_back(times_transposed(grad_branch, proj_back))
    grad_inner = grad_inner_f.astype(BF16)
    grad_proj_in = rows_inner(normed_low, grad_inner)
    grad_in_bias = jnp.sum(grad_inner.astype(F32), axis=0)
    grad_first, grad_norm_one = norm_one_back(grad_second + times_transposed(grad_inner, proj_in))
    grad_attn = grad_first.astype(BF16)
    grad_proj_out = matmul(context_t, grad_attn)
    grad_out_bias = jnp.sum(grad_attn.astype(F32), axis=0)
    grad_context = times_transposed(grad_attn, proj_out).astype(BF16)
    grad_queries_t, grad_keys, grad_values, cells, diag = attention_backward(
        queries, keys, values, grad_context, probs, ops
    )
    table_grad = table_grads(cells, diag)
    grad_mixed = jnp.concatenate([grad_queries_t.T, grad_keys, grad_values], axis=1)
    grad_proj_qkv = rows_inner(start_low, grad_mixed)
    summed = jnp.sum(grad_mixed.astype(F32), axis=0)
    grad_qv_bias = jnp.stack([summed[:D], summed[2 * D :]])
    grad_start = grad_first + times_transposed(grad_mixed, proj_qkv)
    grad_start_low = grad_start.astype(BF16)
    grad_hidden = to_positions(grad_start_low.reshape(1, WINLEN, D))
    grad_proj_box = rows_inner(features, grad_start_low)
    grad_list = (
        grad_proj_qkv,
        grad_proj_out,
        grad_proj_box,
        grad_proj_in,
        grad_proj_back,
        grad_qv_bias,
        grad_out_bias,
        grad_norm_one,
        grad_in_bias,
        grad_back_bias,
        grad_norm_two,
        table_grad,
    )
    padding = jnp.zeros((shard_len * groups * lax.axis_size("dp") - USED,), BF16)
    grads_flat = jnp.concatenate([piece.astype(BF16).reshape(-1) for piece in grad_list] + [padding])
    grad_share = lax.psum_scatter(
        grads_flat, ("dp", "head"), scatter_dimension=0, tiled=True
    ).astype(F32)
    return finish_step(output_low, grad_hidden, grad_share, params, moment_one, moment_two)


def solution(mesh):
    placed = (
        P("dp", "head", None),
        P("dp", "head", None),
        P("dp", None, None),
        P("dp", None),
        P(("dp", "head")),
        P(("dp", "head")),
        P(("dp", "head")),
    )
    return jax.shard_map(
        fast_shards if fits(mesh) else plain_shards,
        mesh=mesh,
        in_specs=placed,
        out_specs=(
            P("dp", "head", None),
            P("dp", "head", None),
            P(("dp", "head")),
            P(("dp", "head")),
            P(("dp", "head")),
        ),
        check_vma=False,
    )
```

profile of v0, /device:TPU:0, one launch (start us, length us, event | category | flops | bytes accessed | tf_op | source)
XLA Modules:
  0.0 253.4 jit_solution(6238324310097624775)
XLA Ops:
  0.6 107.8 %forward_pass.1 = (bf16[768,2304]{1,0:T(8,128)(2,1)}, bf16[768,768]{1,0:T(8,128)(2,1)}, bf16[768,3072]{1,0:T(8,128)(2,1)}, bf16[3072,768]{1,0:T(8,128)(2,1)}, bf...) custom-call(f32[1880,128]{1,0:T(8,128)} %bitcast.6, ...), custom_call_target="tpu_custom_call" | custom-call | tf_op jit(solution)/shard_map/forward_pass/pallas_call | solution.py:1249
  108.4 0.0 copy-start
  108.5 0.0 copy-start.1
  108.5 139.1 %backward_pass.1 = (f32[4,480,128]{2,1,0:T(8,128)}, bf16[4,128,768]{2,1,0:T(8,128)(2,1)}, bf16[4,128,768]{2,1,0:T(8,128)(2,1)}, bf16[12,512,512]{2,1,0:T(8,128)(2,1)}) custom-call(bf16[3072,768]{1,0:T(8,128)(2,1)} %get-tuple-element.27.w_back_in, bf16[768,3072]{1,0:T(8,128)(2,1)} %get-tuple-element.28.w_in_in, bf16[768,768]{1,0:T(8,128)(2,1)} %get-tuple-element.29.w_out_in, ...), custom_call_target="tpu_custom_call" | custom-call | tf_op jit(solution)/shard_map/backward_pass/pallas_call | solution.py:2079
  247.6 0.0 copy-start.2
  247.6 0.0 copy-done
  247.6 0.0 copy-done.1
  247.6 0.0 copy-start.3
  247.6 3.6 %fusion.6 = (f32[240640]{0:T(1024)}, f32[240640]{0:T(1024)}, f32[240640]{0:T(1024)}) fusion(f32[240640]{0:T(1024)S(1)} %copy-done, f32[240640]{0:T(1024)S(1)} %copy-done.1, s32[]{:T(128)S(6)} %mul.40, f32[240640]{0:T(1024)} %param.13, f32[1920,128]{1,0:T(8,128)} %bitcast.7), kind=kLoop, calls=%fused_computation.7 | loop fusion | flops 5294080 | bytes 6737924 | tf_op jit(solution)/shard_map/mul | solution.py:686
  251.2 0.0 copy-done.3
  251.2 0.9 copy.15
  252.1 0.0 copy-done.2
  252.1 0.9 copy.16
Async XLA Ops:
  108.4 139.2 %copy-start = (f32[240640]{0:T(1024)S(1)}, f32[240640]{0:T(1024)}, u32[]{:S(2)}) copy-start(f32[240640]{0:T(1024)} %param.12) | copy-start | bytes 2887684
  108.5 139.2 %copy-start.1 = (f32[240640]{0:T(1024)S(1)}, f32[240640]{0:T(1024)}, u32[]{:S(2)}) copy-start(f32[240640]{0:T(1024)} %param.14) | copy-start | bytes 2887684
  247.6 4.5 %copy-start.2 = (bf16[4,128,768]{2,1,0:T(8,128)(2,1)S(1)}, bf16[4,128,768]{2,1,0:T(8,128)(2,1)}, u32[]{:S(2)}) copy-start(bf16[4,128,768]{2,1,0:T(8,128)(2,1)} %get-tuple-element.58) | copy-start | bytes 2359300
  247.6 3.6 %copy-start.3 = (bf16[4,128,768]{2,1,0:T(8,128)(2,1)S(1)}, bf16[4,128,768]{2,1,0:T(8,128)(2,1)}, u32[]{:S(2)}) copy-start(bf16[4,128,768]{2,1,0:T(8,128)(2,1)} %get-tuple-element.57) | copy-start | bytes 2359300
where the time goes:
time: 257 us; the launch traced here: 253 us
  Pallas kernels  247 us (96%)
  other arithmetic  3.61 us (1%)
    pallas_call x1, Pallas kernels, backward_pass(): pl.pallas_call(functools.partial(backward_kernel, plan), out_shape=[jax.S...  139 us
    pallas_call x1, Pallas kernels, forward_pass(): pl.pallas_call(functools.partial(forward_kernel, plan), out_shape=[shape...  108 us

commit v1 on v0

--- a/solution.py
+++ b/solution.py
@@ -1567,7 +1567,8 @@
     features_t = w_back.at[:D, :WINLEN]
     low_t = w_out.at[:WINLEN]
     scores = [hat.at[:, :WINLEN], scores_odd]
-    dscores = [slope.at[:, :WINLEN], slope.at[:, WINLEN : 2 * WINLEN]]
+    dscores = [w_back.at[2 * WINLEN : 3 * WINLEN, :WINLEN], w_back.at[3 * WINLEN : 4 * WINLEN, :WINLEN]]
+    low_turned = w_back.at[4 * WINLEN : 4 * WINLEN + D, :WINLEN]
     output_low = w_out.at[:WINLEN]
     output_low = w_out.at[:WINLEN]
     dscores_x = [slope.at[:, 2 * WINLEN : 3 * WINLEN], slope.at[:, 3 * WINLEN : 4 * WINLEN]]
@@ -1782,7 +1783,6 @@
         dctx[:, lanes] = times_transposed(grad_attn[...], w_out[lanes, :]).astype(BF16)
     load("low", low_in, low_t)
     loads["context"].wait()
-    in_rows(1, 0, 304)
     reducing.second(2, 0)
     reducing.second(2, 1)
 
@@ -1792,7 +1792,6 @@
             got = matmul(context_t[begin:end, :], grad_attn[:, lanes])
             store(k, 1, begin, got, n * (NBLOCK // LANES))
 
-    out_rows(1, 192, D)
     reducing.fourth(3, 0)
     reducing.fourth(3, 1)
     reducing.give(3, 0)
@@ -1898,37 +1897,43 @@
 
     for odd in range(2):
         spill_copy(0, odd).wait()
+    loads["low"].wait()
+    for n in range(D // NBLOCK):
+        rows = slice(n * NBLOCK, (n + 1) * NBLOCK)
+        low_turned[rows, :] = low_t[:, rows].T
+
+    def qkv_rows(n, carry):
+        lanes = pl.ds(pl.multiple_of(n * NBLOCK, NBLOCK), NBLOCK)
+        store(0, 0, 0, matmul(low_turned[...], mixed[:, lanes]), n * (NBLOCK // LANES))
+        return carry
+
+    lax.fori_loop(0, 3 * D // NBLOCK, qkv_rows, 0)
+    out_rows(0, 0, 208)
+    reducing.settle(2)
+    unstage_column(plan, flat, staged, 0)
+    reducing.swap(0, 0)
+    reducing.swap(0, 1)
+
     loads["w_qkv"].wait()
     for n in range(D // NBLOCK):
         lanes = slice(n * NBLOCK, (n + 1) * NBLOCK)
         value = second[:, lanes] + times_transposed(mixed[...], w_qkv[lanes, :])
         hidden_low[:, lanes] = value.astype(BF16)
     own_hidden = to_pos(hidden_low, hidden_pos, 1)
+    reducing.first(0, 0)
+    reducing.first(0, 1)
     loads["features"].wait()
     for n in range(D // NBLOCK):
         lanes = slice(n * NBLOCK, (n + 1) * NBLOCK)
         store(1, 2, 0, matmul(features_t[...], hidden_low[:, lanes]), n * (NBLOCK // LANES))
+    in_rows(1, 0, 304)
+    out_rows(1, 192, D)
     reducing.settle(3)
     unstage_column(plan, flat, staged, 1)
     reducing.swap(1, 0)
     reducing.swap(1, 1)
-
-    loads["low"].wait()
-    for n in range(D // NBLOCK):
-        rows = slice(n * NBLOCK, (n + 1) * NBLOCK)
-        turned[rows, :] = low_t[:, rows].T
-
-    def qkv_rows(n, carry):
-        lanes = pl.ds(pl.multiple_of(n * NBLOCK, NBLOCK), NBLOCK)
-        store(0, 0, 0, matmul(turned[...], mixed[:, lanes]), n * (NBLOCK // LANES))
-        return carry
-
-    lax.fori_loop(0, 3 * D // NBLOCK, qkv_rows, 0)
-    out_rows(0, 0, 208)
-    reducing.settle(2)
-    unstage_column(plan, flat, staged, 0)
-    reducing.swap(0, 0)
-    reducing.swap(0, 1)
+    reducing.second(0, 0)
+    reducing.second(0, 1)
 
     def fetch_scores(head):
         there = slope.at[:, pl.ds(pl.multiple_of(lax.rem(head, 2) * WINLEN, WINLEN), WINLEN)]
@@ -1976,15 +1981,16 @@
     reducing.first(1, 0)
     reducing.first(1, 1)
     lax.fori_loop(0, 4, one_table, 0)
-    reducing.first(0, 0)
+    reducing.third(0, 0)
     reducing.second(1, 0)
-    reducing.first(0, 1)
+    reducing.third(0, 1)
     reducing.second(1, 1)
     lax.fori_loop(4, 8, one_table, 0)
-    reducing.second(0, 0)
+    reducing.fourth(0, 0)
+    reducing.give(0, 0)
     reducing.third(1, 0)
-    reducing.second(0, 1)
-    reducing.third(1, 1)
+    reducing.fourth(0, 1)
+    reducing.give(0, 1)
     lax.fori_loop(8, HEADS, one_table, 0)
     notes[...] = jnp.zeros_like(notes)
     table = VEC["tables"] // LANES
@@ -1992,18 +1998,13 @@
         notes[row : row + 1, :] = vecg[0:1, row * LANES : (row + 1) * LANES]
     notes[table : table + 9, :] = bucket_rows(cell_rows, diag_rows)
     climbing.start()
-    reducing.third(0, 0)
+    reducing.third(1, 1)
+    climbing.rise()
     reducing.fourth(1, 0)
     reducing.give(1, 0)
-    climbing.rise()
-    reducing.third(0, 1)
+    climbing.end()
     reducing.fourth(1, 1)
     reducing.give(1, 1)
-    reducing.fourth(0, 0)
-    reducing.give(0, 0)
-    climbing.end()
-    reducing.fourth(0, 1)
-    reducing.give(0, 1)
     reducing.receive(out)
     note_quarter, note_first, note_row = note_place(plan)
     base = note_first + note_row

time: 257 us -> 252 us (0.981)
  Pallas kernels: 247 us -> 242 us
    pallas_call x1, Pallas kernels: 139 us -> 134 us  [backward_pass(): pl.pallas_call(functools.partial(backward_kernel, plan), out_shape=[jax.S...]
where the time goes in v1:
time: 252 us; the launch traced here: 248 us
  Pallas kernels  242 us (96%)
  other arithmetic  3.61 us (1%)
    pallas_call x1, Pallas kernels, backward_pass(): pl.pallas_call(functools.partial(backward_kernel, plan), out_shape=[jax.S...  134 us
    pallas_call x1, Pallas kernels, forward_pass(): pl.pallas_call(functools.partial(forward_kernel, plan), out_shape=[shape...  108 us

profile of v1, /device:TPU:0, one launch (start us, length us, event | category | flops | bytes accessed | tf_op | source)
XLA Modules:
  0.0 248.2 jit_solution(16209322676524190465)
XLA Ops:
  0.6 107.8 %forward_pass.1 = (bf16[768,2304]{1,0:T(8,128)(2,1)}, bf16[768,768]{1,0:T(8,128)(2,1)}, bf16[768,3072]{1,0:T(8,128)(2,1)}, bf16[3072,768]{1,0:T(8,128)(2,1)}, bf...) custom-call(f32[1880,128]{1,0:T(8,128)} %bitcast.6, ...), custom_call_target="tpu_custom_call" | custom-call | tf_op jit(solution)/shard_map/forward_pass/pallas_call | solution.py:1249
  108.4 0.0 copy-start
  108.5 0.0 copy-start.1
  108.5 133.9 %backward_pass.1 = (f32[4,480,128]{2,1,0:T(8,128)}, bf16[4,128,768]{2,1,0:T(8,128)(2,1)}, bf16[4,128,768]{2,1,0:T(8,128)(2,1)}, bf16[12,512,512]{2,1,0:T(8,128)(2,1)}) custom-call(bf16[3072,768]{1,0:T(8,128)(2,1)} %get-tuple-element.27.w_back_in, bf16[768,3072]{1,0:T(8,128)(2,1)} %get-tuple-element.28.w_in_in, bf16[768,768]{1,0:T(8,128)(2,1)} %get-tuple-element.29.w_out_in, ...), custom_call_target="tpu_custom_call" | custom-call | tf_op jit(solution)/shard_map/backward_pass/pallas_call | solution.py:2080
  242.3 0.0 copy-start.2
  242.3 0.0 copy-done
  242.4 0.0 copy-done.1
  242.4 0.0 copy-start.3
  242.4 3.6 %fusion.6 = (f32[240640]{0:T(1024)}, f32[240640]{0:T(1024)}, f32[240640]{0:T(1024)}) fusion(f32[240640]{0:T(1024)S(1)} %copy-done, f32[240640]{0:T(1024)S(1)} %copy-done.1, s32[]{:T(128)S(6)} %mul.40, f32[240640]{0:T(1024)} %param.13, f32[1920,128]{1,0:T(8,128)} %bitcast.7), kind=kLoop, calls=%fused_computation.7 | loop fusion | flops 5294080 | bytes 6737924 | tf_op jit(solution)/shard_map/mul | solution.py:686
  246.0 0.0 copy-done.3
  246.0 0.9 copy.15
  246.9 0.0 copy-done.2
  246.9 0.9 copy.16
Async XLA Ops:
  108.4 133.9 %copy-start = (f32[240640]{0:T(1024)S(1)}, f32[240640]{0:T(1024)}, u32[]{:S(2)}) copy-start(f32[240640]{0:T(1024)} %param.12) | copy-start | bytes 2887684
  108.5 133.9 %copy-start.1 = (f32[240640]{0:T(1024)S(1)}, f32[240640]{0:T(1024)}, u32[]{:S(2)}) copy-start(f32[240640]{0:T(1024)} %param.14) | copy-start | bytes 2887684
  242.3 4.5 %copy-start.2 = (bf16[4,128,768]{2,1,0:T(8,128)(2,1)S(1)}, bf16[4,128,768]{2,1,0:T(8,128)(2,1)}, u32[]{:S(2)}) copy-start(bf16[4,128,768]{2,1,0:T(8,128)(2,1)} %get-tuple-element.58) | copy-start | bytes 2359300
  242.4 3.6 %copy-start.3 = (bf16[4,128,768]{2,1,0:T(8,128)(2,1)S(1)}, bf16[4,128,768]{2,1,0:T(8,128)(2,1)}, u32[]{:S(2)}) copy-start(bf16[4,128,768]{2,1,0:T(8,128)(2,1)} %get-tuple-element.57) | copy-start | bytes 2359300

commit v2 on v1

--- a/solution.py
+++ b/solution.py
@@ -1135,11 +1135,11 @@
         return carry
 
     lax.fori_loop(0, 2, one_pair, 0)
+    exchange(cot_in, cot_ref, 1)
     gathering.second(2, 0)
     gathering.first(3, 0)
     gathering.second(2, 1)
     gathering.first(3, 1)
-    exchange(cot_in, cot_ref, 1)
     lax.fori_loop(2, 4, one_pair, 0)
     for h in range(2):
         gathering.third(2, h)

time: 252 us -> 252 us (level)
  no operation moved by 1% of the time
where the time goes in v2:
time: 252 us; the launch traced here: 248 us
  Pallas kernels  242 us (96%)
  other arithmetic  3.61 us (1%)
    pallas_call x1, Pallas kernels, backward_pass(): pl.pallas_call(functools.partial(backward_kernel, plan), out_shape=[jax.S...  134 us
    pallas_call x1, Pallas kernels, forward_pass(): pl.pallas_call(functools.partial(forward_kernel, plan), out_shape=[shape...  108 us

profile of v2, /device:TPU:0, one launch (start us, length us, event | category | flops | bytes accessed | tf_op | source)
XLA Modules:
  0.0 248.4 jit_solution(11454929487956344550)
XLA Ops:
  0.6 107.8 %forward_pass.1 = (bf16[768,2304]{1,0:T(8,128)(2,1)}, bf16[768,768]{1,0:T(8,128)(2,1)}, bf16[768,3072]{1,0:T(8,128)(2,1)}, bf16[3072,768]{1,0:T(8,128)(2,1)}, bf...) custom-call(f32[1880,128]{1,0:T(8,128)} %bitcast.6, ...), custom_call_target="tpu_custom_call" | custom-call | tf_op jit(solution)/shard_map/forward_pass/pallas_call | solution.py:1249
  108.4 0.0 copy-start
  108.5 0.0 copy-start.1
  108.5 134.0 %backward_pass.1 = (f32[4,480,128]{2,1,0:T(8,128)}, bf16[4,128,768]{2,1,0:T(8,128)(2,1)}, bf16[4,128,768]{2,1,0:T(8,128)(2,1)}, bf16[12,512,512]{2,1,0:T(8,128)(2,1)}) custom-call(bf16[3072,768]{1,0:T(8,128)(2,1)} %get-tuple-element.27.w_back_in, bf16[768,3072]{1,0:T(8,128)(2,1)} %get-tuple-element.28.w_in_in, bf16[768,768]{1,0:T(8,128)(2,1)} %get-tuple-element.29.w_out_in, ...), custom_call_target="tpu_custom_call" | custom-call | tf_op jit(solution)/shard_map/backward_pass/pallas_call | solution.py:2080
  242.5 0.0 copy-start.2
  242.5 0.0 copy-done
  242.5 0.0 copy-done.1
  242.5 0.0 copy-start.3
  242.6 3.6 %fusion.6 = (f32[240640]{0:T(1024)}, f32[240640]{0:T(1024)}, f32[240640]{0:T(1024)}) fusion(f32[240640]{0:T(1024)S(1)} %copy-done, f32[240640]{0:T(1024)S(1)} %copy-done.1, s32[]{:T(128)S(6)} %mul.40, f32[240640]{0:T(1024)} %param.13, f32[1920,128]{1,0:T(8,128)} %bitcast.7), kind=kLoop, calls=%fused_computation.7 | loop fusion | flops 5294080 | bytes 6737924 | tf_op jit(solution)/shard_map/mul | solution.py:686
  246.2 0.0 copy-done.3
  246.2 0.9 copy.15
  247.1 0.0 copy-done.2
  247.1 0.9 copy.16
Async XLA Ops:
  108.4 134.1 %copy-start = (f32[240640]{0:T(1024)S(1)}, f32[240640]{0:T(1024)}, u32[]{:S(2)}) copy-start(f32[240640]{0:T(1024)} %param.12) | copy-start | bytes 2887684
  108.5 134.1 %copy-start.1 = (f32[240640]{0:T(1024)S(1)}, f32[240640]{0:T(1024)}, u32[]{:S(2)}) copy-start(f32[240640]{0:T(1024)} %param.14) | copy-start | bytes 2887684
  242.5 4.5 %copy-start.2 = (bf16[4,128,768]{2,1,0:T(8,128)(2,1)S(1)}, bf16[4,128,768]{2,1,0:T(8,128)(2,1)}, u32[]{:S(2)}) copy-start(bf16[4,128,768]{2,1,0:T(8,128)(2,1)} %get-tuple-element.58) | copy-start | bytes 2359300
  242.5 3.6 %copy-start.3 = (bf16[4,128,768]{2,1,0:T(8,128)(2,1)S(1)}, bf16[4,128,768]{2,1,0:T(8,128)(2,1)}, u32[]{:S(2)}) copy-start(bf16[4,128,768]{2,1,0:T(8,128)(2,1)} %get-tuple-element.57) | copy-start | bytes 2359300
